TPU v7x, 512 devices: a whole 4x4x16 slice. The times are simulated.
512 devices in a mesh: seq: 128 (over z, x, core), head: 4 (over y).
Axes of the slice: x: 4, y: 4, z: 16, core: 2. Of those that a mesh axis runs over, the one named last changes fastest.
Arguments:
- tokens: bfloat16 [16384, 1024], P('seq', 'head'), may hold values from -6 to 6
- key_weight: bfloat16 [1024, 1024], P(None, 'head'), may hold values from -0.1875 to 0.1875
- value_weight: bfloat16 [1024, 1024], P(None, 'head'), may hold values from -0.1875 to 0.1875
- buckets: int32 [4, 16, 16384, 1], P(None, 'head', 'seq'), may hold values from 0 to 127; in each aligned block of 128 rows (0 to 127, 128 to 255, ..., all dimensions but the last counted through in order) at most 2 rows name the same one
- cotangent: bfloat16 [16384, 1024], P('seq', 'head'), may hold values from -6 to 6
Outputs:
- attention: float32 [16384, 1024], P('seq', 'head')
- grad_input: float32 [16384, 1024], P('seq', 'head')
Inputs may be any that keep to these rules, and one draw needn't show every extreme that they name: `buckets`: in each round and head, at most 2 of the 128 tokens of one device share a bucket, and this many do in some of them.
All inputs are finite; a program needn't handle non-finite values.
Results may differ from a plain program's by a relative error of at most 0.017.
Values may be sent and summed in bfloat16 or wider, within the bound.
A program may use at most 64 MiB of HBM per device.

v0:
```python
import jax
import jax.numpy as jnp
from jax import lax
from jax.sharding import PartitionSpec as P

sharpness = 16.0


def unit_rows(rows):
    rows_f = rows.astype(jnp.float32)
    length = jnp.sqrt(jnp.sum(rows_f * rows_f, axis=-1, keepdims=True) + 1e-06)
    unit = rows_f / length
    return (unit, unit.astype(jnp.bfloat16), length)


def row_probs(unit_b, valid_rows):
    count = unit_b.shape[0]
    scores = sharpness * jnp.einsum(
        "ihe,jhe->hij", unit_b, unit_b, preferred_element_type=jnp.float32
    )
    diagonal = lax.broadcasted_iota(jnp.int32, (count, count), 0) == lax.broadcasted_iota(
        jnp.int32, (count, count), 1
    )
    columns = valid_rows.astype(jnp.float32).T[:, None, :]
    weights = jnp.where(diagonal[None], 1.0, jnp.exp(scores) * columns)
    totals = jnp.sum(weights, axis=-1)
    return (weights / totals[..., None], totals, diagonal)


def owner_forward(shared_rows, value_rows, valid_rows):
    unit, unit_b, length = unit_rows(shared_rows)
    probs, totals, diagonal = row_probs(unit_b, valid_rows)
    output = jnp.einsum(
        "hij,jhe->ihe", probs.astype(jnp.bfloat16), value_rows, preferred_element_type=jnp.float32
    )
    return (output, jnp.log(totals).T)


def owner_backward(shared_rows, value_rows, valid_rows, grad_rows, offsets):
    unit, unit_b, length = unit_rows(shared_rows)
    probs, totals, diagonal = row_probs(unit_b, valid_rows)
    grad_b = grad_rows.astype(jnp.bfloat16)
    grad_probs = jnp.einsum("ihe,jhe->hij", grad_b, value_rows, preferred_element_type=jnp.float32)
    grad_scores = jnp.where(diagonal[None], 0.0, probs * (grad_probs + offsets.T[:, :, None]))
    scores_b = grad_scores.astype(jnp.bfloat16)
    grad_values = jnp.einsum(
        "hij,ihe->jhe", probs.astype(jnp.bfloat16), grad_b, preferred_element_type=jnp.float32
    )
    grad_unit = sharpness * (
        jnp.einsum("hij,jhe->ihe", scores_b, unit_b, preferred_element_type=jnp.float32)
        + jnp.einsum("hji,jhe->ihe", scores_b, unit_b, preferred_element_type=jnp.float32)
    )
    grad_shared = (grad_unit - unit * jnp.sum(unit * grad_unit, axis=-1, keepdims=True)) / length
    return (grad_shared.astype(jnp.bfloat16), grad_values.astype(jnp.bfloat16))


def to_slots(values, slot_index, round_index, head_index, slot_count):
    shape = (values.shape[0], slot_count, values.shape[1]) + values.shape[3:]
    return jnp.zeros(shape, values.dtype).at[round_index, slot_index, head_index].set(values)


def from_slots(buffer, slot_index, round_index, head_index):
    return buffer[round_index, slot_index, head_index]


def shards(tokens, key_weight, value_weight, buckets, cotangent):
    tok_count = tokens.shape[0]
    devices_seq = lax.axis_size("seq")
    rounds = buckets.shape[0]
    heads_here = buckets.shape[1]
    width_here = key_weight.shape[1]
    head_size = width_here // heads_here
    per_bucket = 2 * tok_count // devices_seq
    slot_count = devices_seq * per_bucket
    piece = lax.all_gather(tokens, "head", axis=1, tiled=True)
    rows = piece.shape[1]
    shared_acc = jnp.dot(piece, key_weight, preferred_element_type=jnp.float32)
    value_acc = jnp.dot(piece, value_weight, preferred_element_type=jnp.float32)
    shared = shared_acc.astype(jnp.bfloat16)
    values = value_acc.astype(jnp.bfloat16)
    bucket_ids = buckets[..., 0]
    onehot = (bucket_ids[..., None] == jnp.arange(devices_seq, dtype=jnp.int32)).astype(jnp.int32)
    ranking = jnp.sum(jnp.cumsum(onehot, axis=2) * onehot, axis=-1) - 1
    slot_index = bucket_ids * per_bucket + ranking
    round_index = jnp.arange(rounds, dtype=jnp.int32)[:, None, None]
    head_index = jnp.arange(heads_here, dtype=jnp.int32)[None, :, None]

    def heads_first(matrix):
        split = matrix.reshape(tok_count, heads_here, head_size).transpose(1, 0, 2)
        return jnp.broadcast_to(split[None], (rounds, heads_here, tok_count, head_size))

    def pack(values_in):
        buffer = to_slots(values_in, slot_index, round_index, head_index, slot_count)
        return buffer.reshape((rounds, devices_seq, per_bucket, -1))

    shared_buf = pack(heads_first(shared))
    value_buf = pack(heads_first(values))
    valid_buf = pack(jnp.ones((rounds, heads_here, tok_count), jnp.bfloat16))
    received = (
        lax.all_to_all(shared_buf, "seq", split_axis=1, concat_axis=1, tiled=True),
        lax.all_to_all(value_buf, "seq", split_axis=1, concat_axis=1, tiled=True),
        lax.all_to_all(valid_buf, "seq", split_axis=1, concat_axis=1, tiled=True),
    )

    def owner_view(parts):
        return (
            parts[0].reshape(rounds, slot_count, heads_here, head_size),
            parts[1].reshape(rounds, slot_count, heads_here, head_size),
            parts[2].reshape(rounds, slot_count, heads_here),
        )

    shared_rows, value_rows, valid_rows = owner_view(received)
    outputs = []
    log_totals = []
    for turn in range(rounds):
        output, log_total = owner_forward(shared_rows[turn], value_rows[turn], valid_rows[turn])
        outputs.append(output)
        log_totals.append(log_total)
    out_buf = jnp.stack(outputs).reshape(rounds, devices_seq, per_bucket, width_here)
    lse_buf = jnp.stack(log_totals).reshape(rounds, devices_seq, per_bucket, heads_here)
    returned = (
        lax.all_to_all(out_buf, "seq", split_axis=1, concat_axis=1, tiled=True),
        lax.all_to_all(lse_buf, "seq", split_axis=1, concat_axis=1, tiled=True),
    )
    round_out = from_slots(
        returned[0].reshape(rounds, slot_count, heads_here, head_size),
        slot_index,
        round_index,
        head_index,
    )
    round_lse = from_slots(
        returned[1].reshape(rounds, slot_count, heads_here), slot_index, round_index, head_index
    )
    combined = jnp.log(jnp.sum(jnp.exp(round_lse), axis=0))
    share = jnp.exp(round_lse - combined[None])
    attention_heads = jnp.sum(share[..., None] * round_out, axis=0)
    attention = attention_heads.transpose(1, 0, 2).reshape(tok_count, width_here)
    cot_heads = (
        cotangent.astype(jnp.float32).reshape(tok_count, heads_here, head_size).transpose(1, 0, 2)
    )
    grad_round = share[..., None] * cot_heads[None]
    offsets = -share * jnp.sum(cot_heads * attention_heads, axis=-1)[None]
    grads_sent = (
        lax.all_to_all(
            pack(grad_round).astype(jnp.bfloat16), "seq", split_axis=1, concat_axis=1, tiled=True
        ).astype(jnp.float32),
        lax.all_to_all(
            pack(offsets).astype(jnp.bfloat16), "seq", split_axis=1, concat_axis=1, tiled=True
        ).astype(jnp.float32),
    )
    shared_rows, value_rows, valid_rows = owner_view(
        (
            lax.all_to_all(shared_buf, "seq", split_axis=1, concat_axis=1, tiled=True),
            lax.all_to_all(value_buf, "seq", split_axis=1, concat_axis=1, tiled=True),
            lax.all_to_all(valid_buf, "seq", split_axis=1, concat_axis=1, tiled=True),
        )
    )
    grad_rows = grads_sent[0].reshape(rounds, slot_count, heads_here, head_size)
    offset_rows = grads_sent[1].reshape(rounds, slot_count, heads_here)
    grad_shared_list = []
    grad_values_list = []
    for turn in range(rounds):
        grad_in, grad_val = owner_backward(
            shared_rows[turn],
            value_rows[turn],
            valid_rows[turn],
            grad_rows[turn],
            offset_rows[turn],
        )
        grad_shared_list.append(grad_in)
        grad_values_list.append(grad_val)
    shared_grad_buf = jnp.stack(grad_shared_list).reshape(
        rounds, devices_seq, per_bucket, width_here
    )
    value_grad_buf = jnp.stack(grad_values_list).reshape(
        rounds, devices_seq, per_bucket, width_here
    )
    grads_home = (
        lax.all_to_all(shared_grad_buf, "seq", split_axis=1, concat_axis=1, tiled=True),
        lax.all_to_all(value_grad_buf, "seq", split_axis=1, concat_axis=1, tiled=True),
    )

    def per_token_sum(buffer):
        rows = from_slots(
            buffer.reshape(rounds, slot_count, heads_here, head_size),
            slot_index,
            round_index,
            head_index,
        )
        summed = jnp.sum(rows.astype(jnp.float32), axis=0).astype(jnp.bfloat16)
        return summed.transpose(1, 0, 2).reshape(tok_count, width_here)

    grad_shared = per_token_sum(grads_home[0])
    grad_values = per_token_sum(grads_home[1])
    partial_value = jnp.einsum(
        "tf,df->td", grad_shared, key_weight, preferred_element_type=jnp.float32
    ) + jnp.einsum("tf,df->td", grad_values, value_weight, preferred_element_type=jnp.float32)
    grad_input = lax.psum_scatter(
        partial_value.astype(jnp.bfloat16), "head", scatter_dimension=1, tiled=True
    ).astype(jnp.float32)
    return (attention, grad_input)


def solution(mesh):
    in_specs = (
        P("seq", "head"),
        P(None, "head"),
        P(None, "head"),
        P(None, "head", "seq", None),
        P("seq", "head"),
    )
    out_specs = (P("seq", "head"), P("seq", "head"))
    return jax.shard_map(shards, mesh=mesh, in_specs=in_specs, out_specs=out_specs, check_vma=False)
```

profile of v0, /device:TPU:6, one launch (start us, length us, event | category | flops | bytes accessed | tf_op | source)
XLA Modules:
  0.0 526.5 jit_solution(321208728744008542)
XLA Ops:
  7.2 1.1 fusion.59
  8.3 4.9 reduce_window_sum.11
  14.3 14.6 %scatter_custom_fusion.1 = bf16[4096]{0:T(1024)(128)(2,1)S(1)} fusion(s32[2048]{0:T(1024)S(1)} %bitcast.224, bf16[2048]{0:T(1024)(128)(2,1)S(1)} %broadcast.226, bf16[]{:T(256)} %constant.11.clone.1), kind=kCustom, calls=%fused_computation.149 | custom fusion | bytes 8194
  30.0 19.4 %all-to-all-start.1 = ((bf16[4,128,2,4]{3,2,0,1:T(2,128)(2,1)}), bf16[4,128,2,4]{3,2,0,1:T(2,128)(2,1)S(1)}, u32[]{:S(2)}, u32[]{:S(2)}) async-start(bf16[4,128,2,4]{3,2,0,1:T(2,128)(2,1)} %copy.374), calls=%async_computation.1 | async-start | bytes 524288 | tf_op jit(solution)/shard_map/all_to_all | solution.py:102
  49.4 12.8 %all_gather.3 = bf16[128,1024]{1,0:T(8,128)(2,1)S(1)} all-gather(bf16[128,256]{1,0:T(8,128)(2,1)S(1)} %copy-done.36), channel_id=1, replica_groups=mesh['seq'=128,'head'=4] {'head'}, dimensions={1}, use_global_device_ids=true | all-gather | bytes 327680 | tf_op jit(solution)/shard_map/all_gather | solution.py:75
  62.8 6.5 %scatter_custom_fusion = bf16[4096,64]{1,0:T(8,128)(2,1)S(1)} fusion(s32[2048]{0:T(1024)S(1)} %bitcast.221, bf16[2048,64]{1,0:T(8,128)(2,1)S(1)} %bitcast.187, bf16[]{:T(256)} %constant.11.clone.1), kind=kCustom, calls=%fused_computation.101 | custom fusion | bytes 524290
  70.0 1.2 copy.370
  71.3 16.0 %all-to-all-start = ((bf16[4,128,2,256]{3,2,0,1:T(2,128)(2,1)}), bf16[4,128,2,256]{3,2,0,1:T(2,128)(2,1)S(1)}, u32[]{:S(2)}, u32[]{:S(2)}) async-start(bf16[4,128,2,256]{3,2,0,1:T(2,128)(2,1)} %copy.370), calls=%async_computation | async-start | bytes 1048576 | tf_op jit(solution)/shard_map/all_to_all | solution.py:100
  87.9 6.1 %scatter_custom_fusion.2 = bf16[4096,64]{1,0:T(8,128)(2,1)S(1)} fusion(s32[2048]{0:T(1024)S(1)} %bitcast.222, bf16[2048,64]{1,0:T(8,128)(2,1)S(1)} %bitcast.188, bf16[]{:T(256)} %constant.11.clone.1), kind=kCustom, calls=%fused_computation.99 | custom fusion | bytes 524290
  94.7 1.2 copy.393
  95.8 24.4 %all-to-all-done = bf16[4,128,2,256]{3,2,0,1:T(2,128)(2,1)S(1)} async-done(((bf16[4,128,2,256]{3,2,0,1:T(2,128)(2,1)}), bf16[4,128,2,256]{3,2,0,1:T(2,128)(2,1)S(1)}, u32[]{:S(2)}, u32[]{:S(2)}) %all-to-all-start) | async-done | bytes 524320 | tf_op jit(solution)/shard_map/all_to_all | solution.py:100
  120.3 7.3 %all-to-all-start.3 = ((bf16[4,128,2,256]{3,2,0,1:T(2,128)(2,1)}), bf16[4,128,2,256]{3,2,0,1:T(2,128)(2,1)S(1)}, u32[]{:S(2)}, u32[]{:S(2)}) async-start(bf16[4,128,2,256]{3,2,0,1:T(2,128)(2,1)} %copy.393), calls=%async_computation.3 | async-start | bytes 1048576 | tf_op jit(solution)/shard_map/all_to_all | solution.py:101
  135.6 1.0 multiply_reduce_fusion.4
  137.7 22.6 %all-to-all-done.3 = bf16[4,128,2,256]{3,2,0,1:T(2,128)(2,1)S(1)} async-done(((bf16[4,128,2,256]{3,2,0,1:T(2,128)(2,1)}), bf16[4,128,2,256]{3,2,0,1:T(2,128)(2,1)S(1)}, u32[]{:S(2)}, u32[]{:S(2)}) %all-to-all-start.3) | async-done | bytes 524320 | tf_op jit(solution)/shard_map/all_to_all | solution.py:101
  167.7 1.5 fusion.97
  170.8 1.1 stack.67
  171.9 1.5 fusion.96
  175.0 1.1 stack.68
  176.1 1.5 fusion.99
  178.1 1.0 copy.389
  179.1 7.0 %all-to-all-start.2 = ((f32[4,128,2,4]{3,2,0,1:T(2,128)}), f32[4,128,2,4]{3,2,0,1:T(2,128)S(1)}, u32[]{:S(2)}, u32[]{:S(2)}) async-start(f32[4,128,2,4]{3,2,0,1:T(2,128)} %copy.389), calls=%async_computation.2 | async-start | bytes 1048576 | tf_op jit(solution)/shard_map/all_to_all | solution.py:123
  186.2 1.3 convolution_bitcast_fusion.3
  188.1 1.5 pad_maximum_fusion
  189.6 1.3 copy.406
  191.0 28.0 %all-to-all-done.2 = f32[4,128,2,4]{3,2,0,1:T(2,128)S(1)} async-done(((f32[4,128,2,4]{3,2,0,1:T(2,128)}), f32[4,128,2,4]{3,2,0,1:T(2,128)S(1)}, u32[]{:S(2)}, u32[]{:S(2)}) %all-to-all-start.2) | async-done | bytes 16416 | tf_op jit(solution)/shard_map/all_to_all | solution.py:123
  219.0 7.0 %all-to-all-start.4 = ((f32[4,128,2,256]{3,2,0,1:T(2,128)}), f32[4,128,2,256]{3,2,0,1:T(2,128)S(1)}, u32[]{:S(2)}, u32[]{:S(2)}) async-start(f32[4,128,2,256]{3,2,0,1:T(2,128)} %copy.406), calls=%async_computation.4 | async-start | bytes 2097152 | tf_op jit(solution)/shard_map/all_to_all | solution.py:122
  226.4 17.4 %gather_fusion = f32[2048]{0:T(1024)S(1)} fusion(f32[4,256,4]{2,1,0:T(8,128)S(1)} %bitcast.178, s32[2048]{0:T(1024)S(1)} %bitcast.174), kind=kCustom, calls=%fused_computation | custom fusion | bytes 40960 | tf_op jit(solution)/shard_map/gather | solution.py:63
  244.5 36.0 %all-to-all-done.4 = f32[4,128,2,256]{3,2,0,1:T(2,128)S(1)} async-done(((f32[4,128,2,256]{3,2,0,1:T(2,128)}), f32[4,128,2,256]{3,2,0,1:T(2,128)S(1)}, u32[]{:S(2)}, u32[]{:S(2)}) %all-to-all-start.4) | async-done | bytes 1048608 | tf_op jit(solution)/shard_map/all_to_all | solution.py:122
  280.6 1.3 copy.407
  281.9 2.8 reshape.231
  284.7 20.2 %gather_fusion.1 = f32[2048,64]{1,0:T(8,128)} fusion(f32[4,256,4,64]{3,2,1,0:T(4,128)S(1)} %reshape.231, s32[2048]{0:T(1024)S(1)} %bitcast.175), kind=kCustom, calls=%fused_computation.1 | custom fusion | bytes 1073152 | tf_op jit(solution)/shard_map/gather | solution.py:63
  304.8 2.6 broadcast_multiply_fusion
  307.6 8.2 %scatter_custom_fusion.4 = f32[4096]{0:T(1024)S(1)} fusion(s32[2048]{0:T(1024)} %bitcast.225, f32[2048]{0:T(1024)S(1)} %bitcast.226, f32[]{:T(128)} %constant.16.clone.1), kind=kCustom, calls=%fused_computation.144 | custom fusion | bytes 16896
  317.0 8.0 %all-to-all-start.6 = ((bf16[4,128,2,4]{3,2,0,1:T(2,128)(2,1)}), bf16[4,128,2,4]{3,2,0,1:T(2,128)(2,1)}, u32[]{:S(2)}, u32[]{:S(2)}) async-start(bf16[4,128,2,4]{3,2,0,1:T(2,128)(2,1)} %copy.415), calls=%async_computation.6 | async-start | bytes 524288 | tf_op jit(solution)/shard_map/all_to_all | solution.py:147
  324.9 6.5 %scatter_custom_fusion.3 = f32[4096,64]{1,0:T(8,128)S(1)} fusion(s32[2048]{0:T(1024)} %bitcast.223, f32[2048,64]{1,0:T(8,128)} %bitcast.184, f32[]{:T(128)} %constant.16.clone.1), kind=kCustom, calls=%fused_computation.90 | custom fusion | bytes 1049088
  331.4 1.1 convert_element_type.250
  332.5 2.3 convert_element_type.220
  334.8 1.2 copy.411
  336.0 10.5 %all-to-all-done.6 = bf16[4,128,2,4]{3,2,0,1:T(2,128)(2,1)} async-done(((bf16[4,128,2,4]{3,2,0,1:T(2,128)(2,1)}), bf16[4,128,2,4]{3,2,0,1:T(2,128)(2,1)}, u32[]{:S(2)}, u32[]{:S(2)}) %all-to-all-start.6) | async-done | bytes 8224 | tf_op jit(solution)/shard_map/all_to_all | solution.py:147
  346.5 6.9 %all-to-all-start.5 = ((bf16[4,128,2,256]{3,2,0,1:T(2,128)(2,1)}), bf16[4,128,2,256]{3,2,0,1:T(2,128)(2,1)S(1)}, u32[]{:S(2)}, u32[]{:S(2)}) async-start(bf16[4,128,2,256]{3,2,0,1:T(2,128)(2,1)} %copy.411), calls=%async_computation.5 | async-start | bytes 1048576 | tf_op jit(solution)/shard_map/all_to_all | solution.py:144
  353.4 1.8 fusion.94
  355.1 1.6 copy.416
  358.1 28.2 %all-to-all-done.5 = bf16[4,128,2,256]{3,2,0,1:T(2,128)(2,1)S(1)} async-done(((bf16[4,128,2,256]{3,2,0,1:T(2,128)(2,1)}), bf16[4,128,2,256]{3,2,0,1:T(2,128)(2,1)S(1)}, u32[]{:S(2)}, u32[]{:S(2)}) %all-to-all-start.5) | async-done | bytes 524320 | tf_op jit(solution)/shard_map/all_to_all | solution.py:144
  386.3 1.0 fusion.92
  387.3 1.1 convert_element_type.221
  388.7 1.3 fusion.27
  391.8 1.3 fusion.24
  394.9 1.3 fusion.25
  400.0 1.0 pad_maximum_fusion.2
  400.9 1.2 copy.442
  402.1 7.4 %all-to-all-start.7 = ((bf16[4,128,2,256]{3,2,0,1:T(2,128)(2,1)}), bf16[4,128,2,256]{3,2,0,1:T(2,128)(2,1)S(1)}, u32[]{:S(2)}, u32[]{:S(2)}) async-start(bf16[4,128,2,256]{3,2,0,1:T(2,128)(2,1)} %copy.442), calls=%async_computation.7 | async-start | bytes 1048576 | tf_op jit(solution)/shard_map/all_to_all | solution.py:179
  409.6 0.9 fusion.53
  410.5 1.1 copy.447
  411.9 1.2 fusion.56
  414.9 1.0 pad_maximum_fusion.3
  415.9 1.2 copy.457
  417.1 25.3 %all-to-all-done.7 = bf16[4,128,2,256]{3,2,0,1:T(2,128)(2,1)S(1)} async-done(((bf16[4,128,2,256]{3,2,0,1:T(2,128)(2,1)}), bf16[4,128,2,256]{3,2,0,1:T(2,128)(2,1)S(1)}, u32[]{:S(2)}, u32[]{:S(2)}) %all-to-all-start.7) | async-done | bytes 524320 | tf_op jit(solution)/shard_map/all_to_all | solution.py:179
  442.4 7.0 %all-to-all-start.8 = ((bf16[4,128,2,256]{3,2,0,1:T(2,128)(2,1)}), bf16[4,128,2,256]{3,2,0,1:T(2,128)(2,1)S(1)}, u32[]{:S(2)}, u32[]{:S(2)}) async-start(bf16[4,128,2,256]{3,2,0,1:T(2,128)(2,1)} %copy.457), calls=%async_computation.8 | async-start | bytes 1048576 | tf_op jit(solution)/shard_map/all_to_all | solution.py:180
  450.4 13.4 %gather_fusion.2 = bf16[2048,64]{1,0:T(8,128)(2,1)S(1)} fusion(bf16[4,256,4,64]{3,2,1,0:T(4,128)(2,1)S(1)} %reshape.234, s32[2048]{0:T(1024)S(1)} %bitcast.176), kind=kCustom, calls=%fused_computation.2 | custom fusion | bytes 548864 | tf_op jit(solution)/shard_map/gather | solution.py:63
  464.4 18.0 %all-to-all-done.8 = bf16[4,128,2,256]{3,2,0,1:T(2,128)(2,1)S(1)} async-done(((bf16[4,128,2,256]{3,2,0,1:T(2,128)(2,1)}), bf16[4,128,2,256]{3,2,0,1:T(2,128)(2,1)S(1)}, u32[]{:S(2)}, u32[]{:S(2)}) %all-to-all-start.8) | async-done | bytes 524320 | tf_op jit(solution)/shard_map/all_to_all | solution.py:180
  483.3 13.4 %gather_fusion.3 = bf16[2048,64]{1,0:T(8,128)(2,1)S(1)} fusion(bf16[4,256,4,64]{3,2,1,0:T(4,128)(2,1)S(1)} %reshape.236, s32[2048]{0:T(1024)S(1)} %bitcast.177), kind=kCustom, calls=%fused_computation.3 | custom fusion | bytes 548864 | tf_op jit(solution)/shard_map/gather | solution.py:63
  497.0 1.0 fusion.28
  498.9 18.9 %reduce-scatter.2.cloned.1.call-done = bf16[128,256]{1,0:T(8,128)(2,1)} async-done(((bf16[128,1024]{1,0:T(8,128)(2,1)}), bf16[128,256]{1,0:T(8,128)(2,1)}) %reduce-scatter.2.cloned.1.call-update) | async-done | bytes 65552 | tf_op jit(solution)/shard_map/reduce_scatter | solution.py:198
  517.7 1.5 convert_element_type.245
  (277 shorter events, 41.8 us)
Async XLA Ops:
  7.2 55.0 %copy-start = (bf16[1024,256]{1,0:T(8,128)(2,1)S(1)}, bf16[1024,256]{1,0:T(8,128)(2,1)}, u32[]{:S(2)}) copy-start(bf16[1024,256]{1,0:T(8,128)(2,1)} %param.6) | copy-start | bytes 1572868
  7.2 6.1 %copy-start.35 = (s32[4,4,128,1]{2,3,1,0:T(1,128)S(1)}, s32[4,4,128,1]{2,3,1,0:T(1,128)}, u32[]{:S(2)}) copy-start(s32[4,4,128,1]{2,3,1,0:T(1,128)} %param.8) | copy-start | bytes 24580
  7.2 6.8 %copy-start.61 = (s32[3]{0:T(128)S(1)}, s32[3]{0:T(128)}, u32[]{:S(2)}) copy-start(s32[3]{0:T(128)} %constant.41) | copy-start | bytes 40
  7.2 6.9 %copy-start.59 = (s32[3]{0:T(128)S(1)}, s32[3]{0:T(128)}, u32[]{:S(2)}) copy-start(s32[3]{0:T(128)} %constant.44) | copy-start | bytes 40
  7.2 6.9 %copy-start.60 = (s32[3]{0:T(128)S(1)}, s32[3]{0:T(128)}, u32[]{:S(2)}) copy-start(s32[3]{0:T(128)} %constant.8) | copy-start | bytes 40
  8.3 41.0 %copy-start.36 = (bf16[128,256]{1,0:T(8,128)(2,1)S(1)}, bf16[128,256]{1,0:T(8,128)(2,1)}, u32[]{:S(2)}) copy-start(bf16[128,256]{1,0:T(8,128)(2,1)} %param.5) | copy-start | bytes 196612
  14.2 48.5 %copy-start.52 = (s32[4,4,128]{2,1,0:T(4,128)}, s32[4,4,128]{2,1,0:T(4,128)S(1)}, u32[]{:S(2)}) copy-start(s32[4,4,128]{2,1,0:T(4,128)S(1)} %get-tuple-element.38) | copy-start | bytes 24580
  14.3 73.7 %copy-start.51 = (s32[4,4,128]{2,1,0:T(4,128)}, s32[4,4,128]{2,1,0:T(4,128)S(1)}, u32[]{:S(2)}) copy-start(s32[4,4,128]{2,1,0:T(4,128)S(1)} %get-tuple-element.39) | copy-start | bytes 24580
  30.0 41.3 %all-to-all-start.1 = ((bf16[4,128,2,4]{3,2,0,1:T(2,128)(2,1)}), bf16[4,128,2,4]{3,2,0,1:T(2,128)(2,1)S(1)}, u32[]{:S(2)}, u32[]{:S(2)}) async-start(bf16[4,128,2,4]{3,2,0,1:T(2,128)(2,1)} %copy.374), calls=%async_computation.1 | async-start | bytes 524288 | tf_op jit(solution)/shard_map/all_to_all | solution.py:102
  69.3 18.0 %copy-start.7 = (bf16[1024,256]{1,0:T(8,128)(2,1)S(1)}, bf16[1024,256]{1,0:T(8,128)(2,1)}, u32[]{:S(2)}) copy-start(bf16[1024,256]{1,0:T(8,128)(2,1)} %param.7) | copy-start | bytes 1572868
  71.3 49.0 %all-to-all-start = ((bf16[4,128,2,256]{3,2,0,1:T(2,128)(2,1)}), bf16[4,128,2,256]{3,2,0,1:T(2,128)(2,1)S(1)}, u32[]{:S(2)}, u32[]{:S(2)}) async-start(bf16[4,128,2,256]{3,2,0,1:T(2,128)(2,1)} %copy.370), calls=%async_computation | async-start | bytes 1048576 | tf_op jit(solution)/shard_map/all_to_all | solution.py:100
  120.3 40.1 %all-to-all-start.3 = ((bf16[4,128,2,256]{3,2,0,1:T(2,128)(2,1)}), bf16[4,128,2,256]{3,2,0,1:T(2,128)(2,1)S(1)}, u32[]{:S(2)}, u32[]{:S(2)}) async-start(bf16[4,128,2,256]{3,2,0,1:T(2,128)(2,1)} %copy.393), calls=%async_computation.3 | async-start | bytes 1048576 | tf_op jit(solution)/shard_map/all_to_all | solution.py:101
  137.7 25.3 %copy-start.22 = (f32[256,4]{1,0:T(8,128)S(1)}, f32[256,4]{1,0:T(8,128)}, u32[]{:S(2)}) copy-start(f32[256,4]{1,0:T(8,128)} %multiply_reduce_fusion.4) | copy-start | bytes 12292
  160.7 4.4 copy-start.30
  160.7 4.4 copy-start.38
  162.2 12.3 %copy-start.19 = (bf16[256,4,64]{0,2,1:T(8,128)(2,1)}, bf16[256,4,64]{0,2,1:T(8,128)(2,1)S(1)}, u32[]{:S(2)}) copy-start(bf16[256,4,64]{0,2,1:T(8,128)(2,1)S(1)} %copy.403) | copy-start | bytes 393220
  162.6 7.7 %copy-start.17 = (bf16[256,4,64]{0,2,1:T(8,128)(2,1)}, bf16[256,4,64]{0,2,1:T(8,128)(2,1)S(1)}, u32[]{:S(2)}) copy-start(bf16[256,4,64]{0,2,1:T(8,128)(2,1)S(1)} %copy.400) | copy-start | bytes 393220
  165.2 1.6 copy-start.53
  165.7 1.3 copy-start.43
  165.7 1.9 copy-start.39
  165.7 1.9 copy-start.55
  169.2 2.7 copy-start.45
  170.3 3.1 copy-start.1
  173.4 2.7 copy-start.47
  174.5 3.1 copy-start.3
  177.6 8.4 %copy-start.15 = (f32[4,256,256]{1,2,0:T(8,128)}, f32[4,256,256]{1,2,0:T(8,128)S(1)}, u32[]{:S(2)}) copy-start(f32[4,256,256]{1,2,0:T(8,128)S(1)} %get-tuple-element.47) | copy-start | bytes 3145732
  177.6 8.5 %copy-start.49 = (f32[4,256]{1,0:T(4,128)}, f32[4,256]{1,0:T(4,128)S(1)}, u32[]{:S(2)}) copy-start(f32[4,256]{1,0:T(4,128)S(1)} %get-tuple-element.46) | copy-start | bytes 12292
  179.1 39.9 %all-to-all-start.2 = ((f32[4,128,2,4]{3,2,0,1:T(2,128)}), f32[4,128,2,4]{3,2,0,1:T(2,128)S(1)}, u32[]{:S(2)}, u32[]{:S(2)}) async-start(f32[4,128,2,4]{3,2,0,1:T(2,128)} %copy.389), calls=%async_computation.2 | async-start | bytes 1048576 | tf_op jit(solution)/shard_map/all_to_all | solution.py:123
  186.2 3.4 copy-start.5
  189.6 36.4 %copy-start.37 = (bf16[128,256]{1,0:T(8,128)(2,1)S(1)}, bf16[128,256]{1,0:T(8,128)(2,1)}, u32[]{:S(2)}) copy-start(bf16[128,256]{1,0:T(8,128)(2,1)} %param.9) | copy-start | bytes 196612
  219.0 61.5 %all-to-all-start.4 = ((f32[4,128,2,256]{3,2,0,1:T(2,128)}), f32[4,128,2,256]{3,2,0,1:T(2,128)S(1)}, u32[]{:S(2)}, u32[]{:S(2)}) async-start(f32[4,128,2,256]{3,2,0,1:T(2,128)} %copy.406), calls=%async_computation.4 | async-start | bytes 2097152 | tf_op jit(solution)/shard_map/all_to_all | solution.py:122
  243.9 36.6 %copy-start.41 = (f32[4,128]{1,0:T(4,128)}, f32[4,128]{1,0:T(4,128)S(1)}, u32[]{:S(2)}) copy-start(f32[4,128]{1,0:T(4,128)S(1)} %log.43) | copy-start | bytes 6148
  304.8 2.7 copy-start.42
  317.0 29.5 %all-to-all-start.6 = ((bf16[4,128,2,4]{3,2,0,1:T(2,128)(2,1)}), bf16[4,128,2,4]{3,2,0,1:T(2,128)(2,1)}, u32[]{:S(2)}, u32[]{:S(2)}) async-start(bf16[4,128,2,4]{3,2,0,1:T(2,128)(2,1)} %copy.415), calls=%async_computation.6 | async-start | bytes 524288 | tf_op jit(solution)/shard_map/all_to_all | solution.py:147
  335.9 52.7 %copy-start.16 = (f32[4,256,256]{1,2,0:T(8,128)S(1)}, f32[4,256,256]{1,2,0:T(8,128)}, u32[]{:S(2)}) copy-start(f32[4,256,256]{1,2,0:T(8,128)} %copy-done.15) | copy-start | bytes 3145732
  335.9 52.7 %copy-start.21 = (bf16[256,4,64]{0,2,1:T(8,128)(2,1)S(1)}, bf16[256,4,64]{0,2,1:T(8,128)(2,1)}, u32[]{:S(2)}) copy-start(bf16[256,4,64]{0,2,1:T(8,128)(2,1)} %copy.394) | copy-start | bytes 393220
  336.0 52.7 %copy-start.50 = (f32[4,256]{1,0:T(4,128)S(1)}, f32[4,256]{1,0:T(4,128)}, u32[]{:S(2)}) copy-start(f32[4,256]{1,0:T(4,128)} %copy-done.49) | copy-start | bytes 12292
  346.5 39.8 %all-to-all-start.5 = ((bf16[4,128,2,256]{3,2,0,1:T(2,128)(2,1)}), bf16[4,128,2,256]{3,2,0,1:T(2,128)(2,1)S(1)}, u32[]{:S(2)}, u32[]{:S(2)}) async-start(bf16[4,128,2,256]{3,2,0,1:T(2,128)(2,1)} %copy.411), calls=%async_computation.5 | async-start | bytes 1048576 | tf_op jit(solution)/shard_map/all_to_all | solution.py:144
  388.7 1.3 copy-start.23
  388.7 1.3 copy-start.34
  388.7 1.3 copy-start.58
  390.5 1.2 copy-start.14
  390.5 1.2 copy-start.20
  390.6 1.2 copy-start.48
  391.8 1.3 copy-start.25
  391.8 1.3 copy-start.33
  391.8 1.3 copy-start.57
  393.6 1.2 copy-start.12
  393.6 1.2 copy-start.18
  394.9 1.3 copy-start.26
  394.9 1.3 copy-start.32
  394.9 1.3 copy-start.56
  396.7 1.2 copy-start.10
  396.7 1.2 copy-start.40
  399.5 10.0 %copy-start.6 = (bf16[4,256,256]{1,2,0:T(8,128)(2,1)S(1)}, bf16[4,256,256]{1,2,0:T(8,128)(2,1)}, u32[]{:S(2)}) copy-start(bf16[4,256,256]{1,2,0:T(8,128)(2,1)} %copy-done.5) | copy-start | bytes 1572868
  399.5 10.0 %copy-start.24 = (bf16[256,4,64]{0,2,1:T(8,128)(2,1)S(1)}, bf16[256,4,64]{0,2,1:T(8,128)(2,1)}, u32[]{:S(2)}) copy-start(bf16[256,4,64]{0,2,1:T(8,128)(2,1)} %copy-done.23) | copy-start | bytes 393220
  400.0 11.9 %copy-start.4 = (bf16[4,256,256]{1,2,0:T(8,128)(2,1)S(1)}, bf16[4,256,256]{1,2,0:T(8,128)(2,1)}, u32[]{:S(2)}) copy-start(bf16[4,256,256]{1,2,0:T(8,128)(2,1)} %copy-done.3) | copy-start | bytes 1572868
  402.1 11.4 %copy-start.2 = (bf16[4,256,256]{1,2,0:T(8,128)(2,1)S(1)}, bf16[4,256,256]{1,2,0:T(8,128)(2,1)}, u32[]{:S(2)}) copy-start(bf16[4,256,256]{1,2,0:T(8,128)(2,1)} %copy-done.1) | copy-start | bytes 1572868
  402.1 40.3 %all-to-all-start.7 = ((bf16[4,128,2,256]{3,2,0,1:T(2,128)(2,1)}), bf16[4,128,2,256]{3,2,0,1:T(2,128)(2,1)S(1)}, u32[]{:S(2)}, u32[]{:S(2)}) async-start(bf16[4,128,2,256]{3,2,0,1:T(2,128)(2,1)} %copy.442), calls=%async_computation.7 | async-start | bytes 1048576 | tf_op jit(solution)/shard_map/all_to_all | solution.py:179
  410.5 3.0 copy-start.27
  410.5 3.7 copy-start.29
  442.4 39.9 %all-to-all-start.8 = ((bf16[4,128,2,256]{3,2,0,1:T(2,128)(2,1)}), bf16[4,128,2,256]{3,2,0,1:T(2,128)(2,1)S(1)}, u32[]{:S(2)}, u32[]{:S(2)}) async-start(bf16[4,128,2,256]{3,2,0,1:T(2,128)(2,1)} %copy.457), calls=%async_computation.8 | async-start | bytes 1048576 | tf_op jit(solution)/shard_map/all_to_all | solution.py:180
  449.4 68.4 %reduce-scatter.2.cloned.1.call-start = ((), (), s32[]{:S(2)}) async-start(), calls=%async_computation.10 | async-start | bytes 327680 | tf_op jit(solution)/shard_map/reduce_scatter | solution.py:198
  483.3 13.6 %copy-start.8 = (bf16[1024,256]{1,0:T(8,128)(2,1)S(1)}, bf16[1024,256]{1,0:T(8,128)(2,1)}, u32[]{:S(2)}) copy-start(bf16[1024,256]{1,0:T(8,128)(2,1)} %param.7) | copy-start | bytes 1572868
  (8 other events, 8.0 us)
Sparse Core Ops, SparseCore 0:
  498.1 19.5 reduce-scatter.1
where the time goes:
time: 536 us; the launch traced here: 526 us
  waiting for transfers between devices  212 us (40%)
  local copies, waits for them, and re-layouts  160 us (30%)
  starting transfers between devices  85.9 us (16%)
  other arithmetic  22.5 us (4%)
  matrix products  17.6 us (3%)
  between operations  16.1 us (3%)
  blocking collectives  12.8 us (2%)
    gather x4, local copies, waits for them, and re-layouts, from_slots(): return buffer[round_index, slot_index, head_index]  64.3 us
    unnamed x136, local copies, waits for them, and re-layouts  46.9 us
    all_to_all x1, waiting for transfers between devices, shards(): lax.all_to_all(out_buf, 'seq', split_axis=1, concat_axis=1, tiled=True)  36 us
    all_to_all x1, waiting for transfers between devices, shards(): lax.all_to_all(pack(grad_round).astype(jnp.bfloat16), 'seq', split_axis=1...  28.2 us
    all_to_all x1, waiting for transfers between devices, shards(): lax.all_to_all(lse_buf, 'seq', split_axis=1, concat_axis=1, tiled=True)  28 us
    all_to_all x1, waiting for transfers between devices, shards(): lax.all_to_all(shared_grad_buf, 'seq', split_axis=1, concat_axis=1, tiled...  25.3 us
    all_to_all x1, waiting for transfers between devices, shards(): lax.all_to_all(shared_buf, 'seq', split_axis=1, concat_axis=1, tiled=True)  24.4 us
    all_to_all x1, waiting for transfers between devices, shards(): lax.all_to_all(value_buf, 'seq', split_axis=1, concat_axis=1, tiled=True)  22.6 us
  transfers between devices with their start and end apart: 10, of which 10 were waited for; matrix products, arithmetic and copies ran while one was open for 17% of the time, Pallas kernels for 0%

commit v1 on v0

v1 whole, which is shorter than its diff:
```python
import jax
import jax.numpy as jnp
from jax import lax
from jax.experimental import pallas as pl
from jax.experimental.pallas import tpu as pltpu

P = jax.sharding.PartitionSpec
MESH = pl.DeviceIdType.MESH
f32, bf16, i32 = jnp.float32, jnp.bfloat16, jnp.int32

SHARP = 16.0
EMPTY = 1024.0
PEERS = 32
ROUNDS = 4
GROUP = 4


def iota(shape, dim):
    return lax.broadcasted_iota(i32, shape, dim)


def low_lanes(shape):
    return iota(shape, 1) % 128 < 64


def swap(x):
    return pltpu.roll(x, 64, 1)


def mm(a, b):
    return lax.dot_general(a, b, (((1,), (0,)), ((), ())), preferred_element_type=f32)


def mm_t(a, b):
    return lax.dot_general(a, b, (((1,), (1,)), ((), ())), preferred_element_type=f32)


def split2(x):
    high = x.astype(bf16)
    return high, (x - high.astype(f32)).astype(bf16)


def rank_codes(ids):
    ids_f = ids.astype(f32)
    columns = jnp.concatenate([ids_f, jnp.zeros((120, 128), f32)], axis=0).T
    before = iota((128, 128), 0) < iota((128, 128), 1)
    code = jnp.zeros((8, 128), f32)
    for r in range(ROUNDS):
        same = (columns[:, r : r + 1] == ids_f[r : r + 1, :]) & before
        rank = jnp.sum(jnp.where(same, 1.0, 0.0), axis=0, keepdims=True)
        code = jnp.where(iota((8, 128), 0) == r, ids_f[r : r + 1, :] + 128.0 * rank, code)
    return code.astype(i32)


def places(codes):
    bucket, rank = codes & 127, codes >> 7
    block = iota((8, 512), 1) >> 7
    slot = bucket * 4 + block
    both = jnp.concatenate([slot[:4].astype(f32), rank[:4].astype(f32)], axis=0)
    columns = []
    for m in range(GROUP):
        tile = both[:, 128 * m : 128 * m + 128]
        columns.append(jnp.concatenate([tile, jnp.zeros((120, 128), f32)], axis=0).T)
    return bucket, rank, slot, jnp.concatenate(columns, axis=0)


def slot_onehot(slot_row):
    return jnp.where(iota((512, 512), 0) == slot_row, 1.0, 0.0).astype(bf16)


def token_onehot(slot_column):
    return jnp.where(iota((512, 512), 1).astype(f32) == slot_column, 1.0, 0.0).astype(bf16)


def half_mask(rank_column):
    half = (iota((512, 128), 1) >> 6).astype(f32)
    return jnp.where(half == rank_column, 1.0, 0.0).astype(bf16)


def twice(pair):
    pair = pair.astype(f32)
    turned = swap(pair)
    low = low_lanes(pair.shape)
    return jnp.where(low, pair, turned).astype(bf16), jnp.where(low, turned, pair).astype(bf16)


def pack(onehot, rows, mask):
    right = jnp.concatenate([rows[0] * mask, rows[1] * mask, rows[2] * mask, mask], axis=1)
    out = mm(onehot, right)
    filled = out[:, 384:512] > 0.5
    return (
        out[:, 0:128].astype(bf16),
        out[:, 128:256].astype(bf16),
        jnp.where(filled, out[:, 256:384], EMPTY).astype(bf16),
    )


def regroup():
    p, c = iota((128, 128), 0), iota((128, 128), 1)
    hit = ((c >> 4) == ((p & 31) >> 2)) & (((c & 15) >> 2) == (p >> 5)) & ((c & 3) == (p & 3))
    return jnp.where(hit, 1.0, 0.0).astype(bf16)


def regroup_back():
    c, p = iota((128, 128), 0), iota((128, 128), 1)
    hit = ((c >> 4) == ((p & 31) >> 2)) & (((c & 15) >> 2) == (p >> 5)) & ((c & 3) == (p & 3))
    return jnp.where(hit, 1.0, 0.0).astype(bf16)


def half_ones():
    r, c = iota((256, 128), 0), iota((256, 128), 1)
    return jnp.where(((r & 127) >> 6) == (c >> 6), 1.0, 0.0).astype(bf16)


def half_sums(x, ones):
    high, low = split2(x)
    return mm(jnp.concatenate([high, low], axis=1), ones)


def on_rows(x):
    return jnp.concatenate([x, swap(x)], axis=0)


def on_rows_low(x):
    low = low_lanes(x.shape)
    return jnp.concatenate([jnp.where(low, x, 0.0), jnp.where(low, swap(x), 0.0)], axis=0)


def on_diagonal(x):
    low, turned = low_lanes(x.shape), swap(x)
    return jnp.concatenate(
        [jnp.where(low, x, 0.0), jnp.where(low, turned, 0.0), jnp.where(low, 0.0, turned), jnp.where(low, 0.0, x)],
        axis=0,
    ).astype(bf16)


def side_by_side(x):
    return jnp.concatenate([x[:128], x[128:]], axis=1)


def diagonal():
    return iota((256, 256), 0) == iota((256, 256), 1)


def owner_forward(shared, values, cot, ones):
    shared, values, cot = shared.astype(f32), values.astype(f32), cot.astype(f32)
    scale = lax.rsqrt(half_sums(shared * shared, ones) + 1e-6)
    unit = shared * scale
    scores = mm_t(on_rows_low(unit).astype(bf16), on_rows(unit).astype(bf16))
    weights = jnp.where(diagonal(), 1.0, jnp.exp(SHARP * scores))
    low = low_lanes((128, 128))
    valid = jnp.where(cot < 0.5 * EMPTY, 1.0, 0.0)
    turned = swap(valid)
    valid = jnp.concatenate([jnp.where(low, valid, turned), jnp.where(low, turned, valid)], axis=0)
    valid = jnp.concatenate([valid, valid], axis=1)
    totals = jnp.sum(weights * valid, axis=0, keepdims=True)
    along = mm_t(on_rows_low(values).astype(bf16), on_rows(cot).astype(bf16))
    products = jnp.sum(weights * along, axis=0, keepdims=True)
    numerator = mm(side_by_side(weights.astype(bf16)), on_diagonal(values))
    return weights, unit, scale, numerator.astype(bf16), totals, products


def owner_backward(weights, unit, scale, values, cot, rows, columns, ones):
    values, cot = values.astype(f32), cot.astype(f32)
    inv_row, along_row = rows
    wide = [jnp.broadcast_to(c, (128, 128)) for c in columns]
    inv_col = jnp.concatenate([wide[0], wide[1]], axis=0)
    along_col = jnp.concatenate([wide[2], wide[3]], axis=0)
    inv_col = jnp.concatenate([inv_col, inv_col], axis=1)
    along_col = jnp.concatenate([along_col, along_col], axis=1)
    value_rows, cot_rows = on_rows_low(values).astype(bf16), on_rows(cot).astype(bf16)
    right_left = mm_t(value_rows, cot_rows)
    left_right = mm_t(cot_rows, value_rows)
    inner = inv_row * (right_left - along_row) + inv_col * (left_right - along_col)
    grad = jnp.where(diagonal(), 0.0, weights * inner).astype(bf16)
    grad_unit = SHARP * mm(side_by_side(grad), on_diagonal(unit))
    low = low_lanes((128, 128))
    grad_round = jnp.where(low, wide[0], wide[1]) * cot
    grad_values = mm(side_by_side(weights.astype(bf16)), on_diagonal(grad_round))
    grad_shared = (grad_unit - unit * half_sums(unit * grad_unit, ones)) * scale
    return grad_shared.astype(bf16), grad_values.astype(bf16)


def square(x):
    return jnp.concatenate([x, jnp.zeros((128 - x.shape[0], 128), f32)], axis=0)


def place_onehot(bucket_row, block_row):
    return jnp.where(iota((128, 512), 0) == (bucket_row >> 2) * 4 + block_row, 1.0, 0.0).astype(bf16)


def token_scalars(turned, bucket, rank):
    block = iota((1, 512), 1) >> 7
    total, product = jnp.zeros((1, 512), f32), jnp.zeros((1, 512), f32)
    for r in range(ROUNDS):
        onehot = place_onehot(bucket[r : r + 1], block)
        high, low = split2(turned[16 * r : 16 * r + 16])
        picked = mm(jnp.concatenate([high, low], axis=1), jnp.concatenate([onehot, onehot], axis=0))
        hit = iota((8, 512), 0) == rank[r : r + 1] * 4 + (bucket[r : r + 1] & 3)
        total = total + jnp.sum(jnp.where(hit, picked[0:8], 0.0), axis=0, keepdims=True)
        product = product + jnp.sum(jnp.where(hit, picked[8:16], 0.0), axis=0, keepdims=True)
    inverse = 1.0 / total
    return inverse, product * inverse


def spread_scalars(inverse, along, bucket, rank):
    block = iota((1, 512), 1) >> 7
    out = []
    for r in range(ROUNDS):
        onehot = place_onehot(bucket[r : r + 1], block)
        hit = iota((8, 512), 0) == rank[r : r + 1] * 4 + (bucket[r : r + 1] & 3)
        left = jnp.concatenate([jnp.where(hit, inverse, 0.0), jnp.where(hit, along, 0.0)], axis=0)
        high, low = split2(left)
        both = mm_t(jnp.concatenate([high, low], axis=0), onehot)
        out.append(both[0:16] + both[16:32])
    return square(jnp.concatenate(out, axis=0))


def kernel(
    tok, kw, vw, ids, cot, att_out, gin_out,
    gat, wcat, sv_send, cot_send, code_send, sv_land, cot_land, code_land,
    onehot, onehot_t, masks, rows_x, slots_out, slots_in, tasks,
    w_keep, unit_keep, scale_keep, num_task, num_out, num_in, grad_task, grad_out, grad_in,
    z_rows, z_turn, z_out, z_in, q_turn, q_cols, q_out, q_in, acc,
    back_send, back_land, atth_send, atth_land, rs_send, rs_land,
    s0, r0, s1, r1, s2, r2, sn, rn, sg, rg, s3, r3, s4, r4, s6, r6, s7, r7,
):
    seq, y = lax.axis_index("seq"), lax.axis_index("head")
    z, xc = lax.div(seq, 8), lax.rem(seq, 8)
    zq, zr = lax.div(z, 4), lax.rem(z, 4)
    me = xc * 4 + y

    def slab(d):
        return (z * 8 + lax.div(d, 4), lax.rem(d, 4))

    def partner(i):
        return ((4 * i + y) * 8 + xc, zr)

    def arrived(ref, sem):
        pltpu.make_async_copy(ref, ref, sem).wait()

    def to_partner(i, src, land, send_sem, recv_sem):
        @pl.when(4 * i + y == z)
        def _():
            pltpu.make_async_copy(src, land.at[zq], recv_sem.at[zq]).start()

        @pl.when(4 * i + y != z)
        def _():
            pltpu.make_async_remote_copy(
                src, land.at[zq], send_sem.at[i], recv_sem.at[zq], device_id=partner(i), device_id_type=MESH
            ).start()

    def partner_sent(i, src, send_sem):
        @pl.when(4 * i + y != z)
        def _():
            arrived(src, send_sem.at[i])

    def to_slab(out_at, in_at, send_sem, recv_sem):
        pltpu.make_async_copy(out_at(me), in_at(me), recv_sem).start()

        def send(o, carry):
            d = lax.rem(me + o, PEERS)
            pltpu.make_async_remote_copy(
                out_at(d), in_at(me), send_sem, recv_sem, device_id=slab(d), device_id_type=MESH
            ).start()
            return carry

        lax.fori_loop(1, PEERS, send, 0)

    barrier = pltpu.get_barrier_semaphore()

    def greet(o, carry):
        pl.semaphore_signal(barrier, 1, device_id=slab(lax.rem(me + o, PEERS)), device_id_type=MESH)
        return carry

    lax.fori_loop(1, PEERS, greet, 0)
    for i in range(GROUP):

        @pl.when(4 * i + y != z)
        def _(i=i):
            pl.semaphore_signal(barrier, 1, device_id=partner(i), device_id_type=MESH)

    for k in range(GROUP):
        code_send[k] = rank_codes(ids[k])
    low64 = low_lanes((64, 128))
    for k in range(0, GROUP, 2):
        tile = cot[:, 64 * k : 64 * k + 128].astype(f32)
        top, bottom = tile[:64], tile[64:]
        cot_send[k] = jnp.where(low64, top, swap(bottom)).astype(bf16)
        cot_send[k + 1] = jnp.where(low64, swap(top), bottom).astype(bf16)

    pl.semaphore_wait(barrier, jnp.where(zr == y, 34, 35))

    for o in range(1, 4):
        pltpu.make_async_remote_copy(
            tok, gat.at[y], s0.at[o - 1], r0.at[o - 1], device_id=(seq, lax.rem(y + o, 4)), device_id_type=MESH
        ).start()
    for k in range(GROUP):
        to_partner(k, code_send.at[k], code_land, s1.at[0], r1.at[0])
        to_partner(k, cot_send.at[k], cot_land, s1.at[1], r1.at[1])

    def weave(c, carry):
        at = pl.ds(pl.multiple_of(c * 128, 128), 128)
        low = low_lanes((128, 128))
        for k in range(0, GROUP, 2):
            key, value = kw[at, 64 * k : 64 * k + 128].astype(f32), vw[at, 64 * k : 64 * k + 128].astype(f32)
            wcat[at, 128 * k : 128 * k + 128] = jnp.where(low, key, swap(value)).astype(bf16)
            wcat[at, 128 * k + 128 : 128 * k + 256] = jnp.where(low, swap(key), value).astype(bf16)
        return carry

    lax.fori_loop(0, 8, weave, 0)

    project = mm(tok[...], wcat[pl.ds(pl.multiple_of(y * 256, 256), 256), :])
    for o in range(1, 4):
        source = lax.rem(y + 4 - o, 4)
        arrived(gat.at[source], r0.at[o - 1])
        project = project + mm(gat[source], wcat[pl.ds(pl.multiple_of(source * 256, 256), 256), :])
    for k in range(GROUP):
        sv_send[k] = project[:, 128 * k : 128 * k + 128].astype(bf16)
        to_partner(k, sv_send.at[k], sv_land, s1.at[2], r1.at[2])

    for m in range(GROUP):
        arrived(code_land.at[m], r1.at[0, m])
    codes = jnp.concatenate([code_land[m] for m in range(GROUP)], axis=1)
    bucket, rank, slot, columns = places(codes)
    for r in range(ROUNDS):
        onehot[r] = slot_onehot(slot[r : r + 1])
        masks[r] = half_mask(columns[:, 4 + r : 5 + r])
    for m in range(GROUP):
        arrived(cot_land.at[m], r1.at[1, m])
        piece = cot_land[m].astype(f32)
        turned = swap(piece)
        rows_x[2, 128 * m : 128 * m + 64, :] = jnp.where(low64, piece, turned).astype(bf16)
        rows_x[2, 128 * m + 64 : 128 * m + 128, :] = jnp.where(low64, turned, piece).astype(bf16)
    for m in range(GROUP):
        arrived(sv_land.at[m], r1.at[2, m])
        first, second = twice(sv_land[m])
        rows_x[0, 128 * m : 128 * m + 128, :] = first
        rows_x[1, 128 * m : 128 * m + 128, :] = second

    def send_round(r, carry):
        parts = pack(onehot[r], (rows_x[0], rows_x[1], rows_x[2]), masks[r])
        for a in range(3):
            slots_out[r, a] = parts[a]
        to_slab(
            lambda d: slots_out.at[r, :, pl.ds(pl.multiple_of(d * 16, 16), 16), :],
            lambda d: slots_in.at[r, :, pl.ds(pl.multiple_of(d * 16, 16), 16), :],
            s2.at[r],
            r2.at[r],
        )
        return carry

    lax.fori_loop(0, ROUNDS, send_round, 0)

    for r in range(ROUNDS):
        onehot_t[r] = token_onehot(columns[:, r : r + 1])

    ones = half_ones()
    sort, unsort = regroup(), regroup_back()
    z_rows[...] = jnp.zeros((128, 128), f32)

    def forward_round(r, carry):
        arrived(slots_in.at[r], r2.at[r])
        for g in range(4):
            at = slice(128 * g, 128 * g + 128)
            moved = mm(sort, jnp.concatenate([slots_in[r, a, at, :] for a in range(3)], axis=1)).astype(bf16)
            for b in range(GROUP):
                for a in range(3):
                    tasks[r * 4 + b, a, 32 * g : 32 * g + 32, :] = moved[32 * b : 32 * b + 32, 128 * a : 128 * a + 128]

        def one(b, inner):
            t = r * 4 + b
            weights, unit, scale, numerator, totals, products = owner_forward(tasks[t, 0], tasks[t, 1], tasks[t, 2], ones)
            w_keep[t] = weights
            unit_keep[t] = unit
            scale_keep[t] = scale
            num_task[b] = numerator
            line = r * 16 + b
            z_rows[pl.ds(line, 1), :] = totals[:, :128]
            z_rows[pl.ds(line + 4, 1), :] = totals[:, 128:]
            z_rows[pl.ds(line + 8, 1), :] = products[:, :128]
            z_rows[pl.ds(line + 12, 1), :] = products[:, 128:]
            return inner

        lax.fori_loop(0, GROUP, one, 0)
        for g in range(4):
            moved = jnp.concatenate([num_task[b, 32 * g : 32 * g + 32, :] for b in range(GROUP)], axis=0)
            num_out[r, 128 * g : 128 * g + 128, :] = mm(unsort, moved).astype(bf16)
        to_slab(
            lambda d: num_out.at[r, pl.ds(pl.multiple_of(d * 16, 16), 16), :],
            lambda d: num_in.at[r, pl.ds(pl.multiple_of(d * 16, 16), 16), :],
            sn.at[r],
            rn.at[r],
        )
        return carry

    lax.fori_loop(0, ROUNDS, forward_round, 0)

    z_turn[...] = z_rows[...].T
    for d in range(PEERS):
        z_out[d] = z_turn[4 * d : 4 * d + 4, :]
    to_slab(lambda d: z_out.at[d], lambda d: z_in.at[d], s3.at[0], r3.at[0])
    arrived(z_in, r3.at[0])
    for d in range(PEERS):
        q_turn[4 * d : 4 * d + 4, :] = z_in[d]
    inverse, along = token_scalars(q_turn[...].T, bucket, rank)
    z_turn[...] = spread_scalars(inverse, along, bucket, rank).T
    for d in range(PEERS):
        q_out[d] = z_turn[4 * d : 4 * d + 4, :]
    to_slab(lambda d: q_out.at[d], lambda d: q_in.at[d], s4.at[0], r4.at[0])

    acc[:, 0:128] = jnp.zeros((512, 128), f32)

    def gather_out(r, carry):
        arrived(num_in.at[r], rn.at[r])
        acc[:, 0:128] += mm(onehot_t[r], num_in[r]) * masks[r].astype(f32)
        return carry

    lax.fori_loop(0, ROUNDS, gather_out, 0)
    low = low_lanes((128, 128))
    for m in range(GROUP):
        part = acc[128 * m : 128 * m + 128, 0:128]
        inv_col = jnp.broadcast_to(inverse[:, 128 * m : 128 * m + 128], (128, 128)).T
        result = (part + swap(part)) * inv_col
        atth_send[m] = jnp.where(low64, result[:64], result[64:]).astype(bf16)
        to_partner(m, atth_send.at[m], atth_land, s6.at[0], r6.at[0])

    arrived(q_in, r4.at[0])
    for d in range(PEERS):
        q_cols[4 * d : 4 * d + 4, :] = q_in[d]
    q_turn[...] = q_cols[...].T

    def backward_round(r, carry):
        def one(b, inner):
            t = r * 4 + b
            line = r * 16 + b
            near = pltpu.roll(q_cols[...], lax.rem(128 - line, 128), 1)
            rows = [
                jnp.concatenate([q_turn[pl.ds(line + s, 1), :], q_turn[pl.ds(line + s + 4, 1), :]], axis=1)
                for s in (0, 8)
            ]
            cols = [near[:, c : c + 1] for c in (0, 4, 8, 12)]
            grad_shared, grad_values = owner_backward(
                w_keep[t], unit_keep[t], scale_keep[t], tasks[t, 1], tasks[t, 2], rows, cols, ones
            )
            grad_task[b, 0] = grad_shared
            grad_task[b, 1] = grad_values
            return inner

        lax.fori_loop(0, GROUP, one, 0)
        for g in range(4):
            moved = [
                jnp.concatenate([grad_task[b, a, 32 * g : 32 * g + 32, :] for b in range(GROUP)], axis=0) for a in range(2)
            ]
            back = mm(unsort, jnp.concatenate(moved, axis=1)).astype(bf16)
            for a in range(2):
                grad_out[r, a, 128 * g : 128 * g + 128, :] = back[:, 128 * a : 128 * a + 128]
        to_slab(
            lambda d: grad_out.at[r, :, pl.ds(pl.multiple_of(d * 16, 16), 16), :],
            lambda d: grad_in.at[r, :, pl.ds(pl.multiple_of(d * 16, 16), 16), :],
            sg.at[r],
            rg.at[r],
        )
        return carry

    lax.fori_loop(0, ROUNDS, backward_round, 0)

    for k in range(GROUP):
        arrived(atth_land.at[k], r6.at[0, k])
    for k in range(0, GROUP, 2):
        first, second = atth_land[k].astype(f32), atth_land[k + 1].astype(f32)
        att_out[0:64, 64 * k : 64 * k + 128] = jnp.where(low64, first, swap(second))
        att_out[64:128, 64 * k : 64 * k + 128] = jnp.where(low64, swap(first), second)

    acc[...] = jnp.zeros((512, 256), f32)

    def gather_grads(r, carry):
        arrived(grad_in.at[r], rg.at[r])
        got = mm(onehot_t[r], jnp.concatenate([grad_in[r, 0], grad_in[r, 1]], axis=1))
        mask = masks[r].astype(f32)
        acc[...] += got * jnp.concatenate([mask, mask], axis=1)
        return carry

    lax.fori_loop(0, ROUNDS, gather_grads, 0)
    for m in range(GROUP):
        part = acc[128 * m : 128 * m + 128, :]
        first, second = part[:, :128], part[:, 128:]
        back_send[m] = jnp.where(low, first + swap(first), second + swap(second)).astype(bf16)
        to_partner(m, back_send.at[m], back_land, s6.at[1], r6.at[1])
    for k in range(GROUP):
        arrived(back_land.at[k], r6.at[1, k])

    left = jnp.concatenate([back_land[k] for k in range(GROUP)], axis=1)
    for o in range(1, 4):
        d = lax.rem(y + o, 4)
        rs_send[o - 1] = mm_t(left, wcat[pl.ds(pl.multiple_of(d * 256, 256), 256), :]).astype(bf16)
        pltpu.make_async_remote_copy(
            rs_send.at[o - 1], rs_land.at[o - 1], s7.at[o - 1], r7.at[o - 1], device_id=(seq, d), device_id_type=MESH
        ).start()
    total = mm_t(left, wcat[pl.ds(pl.multiple_of(y * 256, 256), 256), :])
    for o in range(1, 4):
        arrived(rs_land.at[o - 1], r7.at[o - 1])
        total = total + rs_land[o - 1].astype(f32)
    gin_out[...] = total

    for o in range(3):
        arrived(tok, s0.at[o])
        arrived(rs_send.at[o], s7.at[o])
    for k in range(GROUP):
        partner_sent(k, code_send.at[k], s1.at[0])
        partner_sent(k, cot_send.at[k], s1.at[1])
        partner_sent(k, sv_send.at[k], s1.at[2])
        partner_sent(k, atth_send.at[k], s6.at[0])
        partner_sent(k, back_send.at[k], s6.at[1])
    rest = pl.ds(0, 16 * (PEERS - 1))
    for r in range(ROUNDS):
        arrived(slots_out.at[r, :, rest, :], s2.at[r])
        arrived(num_out.at[r, rest, :], sn.at[r])
        arrived(grad_out.at[r, :, rest, :], sg.at[r])
    arrived(z_out.at[pl.ds(0, PEERS - 1)], s3.at[0])
    arrived(q_out.at[pl.ds(0, PEERS - 1)], s4.at[0])


def shards(tokens, key_weight, value_weight, buckets, cotangent):
    ids = jnp.pad(buckets[..., 0].transpose(1, 0, 2), ((0, 0), (0, 4), (0, 0)))
    vmem = pl.BlockSpec(memory_space=pltpu.VMEM)
    v, dma = pltpu.VMEM, pltpu.SemaphoreType.DMA
    scratch = [
        v((4, 128, 256), bf16),
        v((1024, 512), bf16),
        v((4, 128, 128), bf16),
        v((4, 64, 128), bf16),
        v((4, 8, 128), i32),
        v((4, 128, 128), bf16),
        v((4, 64, 128), bf16),
        v((4, 8, 128), i32),
        v((4, 512, 512), bf16),
        v((4, 512, 512), bf16),
        v((4, 512, 128), bf16),
        v((3, 512, 128), bf16),
        v((4, 3, 512, 128), bf16),
        v((4, 3, 512, 128), bf16),
        v((16, 3, 128, 128), bf16),
        v((16, 256, 256), f32),
        v((16, 128, 128), f32),
        v((16, 128, 128), f32),
        v((4, 128, 128), bf16),
        v((4, 512, 128), bf16),
        v((4, 512, 128), bf16),
        v((4, 2, 128, 128), bf16),
        v((4, 2, 512, 128), bf16),
        v((4, 2, 512, 128), bf16),
        v((128, 128), f32),
        v((128, 128), f32),
        v((32, 4, 128), f32),
        v((32, 4, 128), f32),
        v((128, 128), f32),
        v((128, 128), f32),
        v((32, 4, 128), f32),
        v((32, 4, 128), f32),
        v((512, 256), f32),
        v((4, 128, 128), bf16),
        v((4, 128, 128), bf16),
        v((4, 64, 128), bf16),
        v((4, 64, 128), bf16),
        v((3, 128, 256), bf16),
        v((3, 128, 256), bf16),
        dma((3,)), dma((3,)),
        dma((3, 4)), dma((3, 4)),
        dma((4,)), dma((4,)),
        dma((4,)), dma((4,)),
        dma((4,)), dma((4,)),
        dma((1,)), dma((1,)),
        dma((1,)), dma((1,)),
        dma((2, 4)), dma((2, 4)),
        dma((3,)), dma((3,)),
    ]
    return pl.pallas_call(
        kernel,
        out_shape=(jax.ShapeDtypeStruct((128, 256), f32), jax.ShapeDtypeStruct((128, 256), f32)),
        in_specs=[vmem] * 5,
        out_specs=(vmem, vmem),
        scratch_shapes=scratch,
        compiler_params=pltpu.CompilerParams(
            collective_id=0, has_side_effects=True, vmem_limit_bytes=50 * 1024 * 1024
        ),
    )(tokens, key_weight, value_weight, ids, cotangent)


def solution(mesh):
    in_specs = (
        P("seq", "head"),
        P(None, "head"),
        P(None, "head"),
        P(None, "head", "seq", None),
        P("seq", "head"),
    )
    out_specs = (P("seq", "head"), P("seq", "head"))
    return jax.shard_map(shards, mesh=mesh, in_specs=in_specs, out_specs=out_specs, check_vma=False)
```

time: 536 us -> 114 us (0.21); the launches traced: 526 us -> 112 us
  waiting for transfers between devices: 212 us -> 0 us
  local copies, waits for them, and re-layouts: 160 us -> 5.78 us
  Pallas kernels: 0 us -> 105 us
  starting transfers between devices: 85.9 us -> 0 us
  other arithmetic: 22.5 us -> 0 us
  matrix products: 17.6 us -> 0 us
  between operations: 16.1 us -> 0.64 us
  blocking collectives: 12.8 us -> 0 us
    all_to_all x9 -> x0, waiting for transfers between devices: 193 us -> none  [the longest x1 36 us: shards(): lax.all_to_all(out_buf, 'seq', split_axis=1, concat_axis=1, tiled=True)]
    pallas_call x0 -> x1, Pallas kernels: none -> 105 us  [shards(): pl.pallas_call(kernel, out_shape=(jax.ShapeDtypeStruct((128, 256), f32),...]
    all_to_all x9 -> x0, starting transfers between devices: 85.8 us -> none  [the longest x1 19.4 us: shards(): lax.all_to_all(valid_buf, 'seq', split_axis=1, concat_axis=1, tiled=True)]
    gather x4 -> x0, local copies, waits for them, and re-layouts: 64.3 us -> none  [from_slots(): return buffer[round_index, slot_index, head_index]]
    unnamed x136 -> x11, local copies, waits for them, and re-layouts: 46.9 us -> 5.77 us
    reduce_scatter x1 -> x0, waiting for transfers between devices: 18.9 us -> none  [shards(): lax.psum_scatter(partial_value.astype(jnp.bfloat16), 'head', scatter_dime...]
    dot_general x28 -> x0, matrix products: 17.6 us -> none  [the longest x4 5.03 us: row_probs(): jnp.einsum('ihe,jhe->hij', unit_b, unit_b, preferred_element_type=jnp.flo...]
    convert_element_type x31 -> x0, local copies, waits for them, and re-layouts: 14.9 us -> none  [the longest x8 5.34 us: unit_rows(): rows_f = rows.astype(jnp.float32)]
  transfers between devices with their start and end apart: 10 -> 0, of which waited for: 10 -> 0; matrix products, arithmetic and copies ran while one was open for 17% -> 0% of each run, Pallas kernels for 0% -> 0%
where the time goes in v1:
time: 114 us; the launch traced here: 112 us
  Pallas kernels  105 us (92%)
  local copies, waits for them, and re-layouts  5.78 us (5%)
    pallas_call x1, Pallas kernels, shards(): pl.pallas_call(kernel, out_shape=(jax.ShapeDtypeStruct((128, 256), f32),...  105 us
    unnamed x11, local copies, waits for them, and re-layouts  5.77 us

profile of v1, /device:TPU:6, one launch (start us, length us, event | category | flops | bytes accessed | tf_op | source)
XLA Modules:
  0.0 111.6 jit_solution(5953161806839319300)
XLA Ops:
  0.6 0.7 copy.9
  1.3 0.0 copy-start
  1.3 1.0 copy-done
  2.4 0.0 copy-start.1
  2.4 1.0 copy-done.1
  3.4 0.0 copy-start.2
  3.4 0.8 copy-done.2
  4.3 0.0 copy-start.3
  4.3 0.8 copy-done.3
  5.1 105.1 %shard_map.68 = (f32[128,256]{1,0:T(8,128)S(1)}, f32[128,256]{1,0:T(8,128)S(1)}) custom-call(bf16[128,256]{1,0:T(8,128)(2,1)S(1)} %copy-done.2, bf16[1024,256]{1,0:T(8,128)(2,1)S(1)} %copy-done, bf16[1024,256]{1,0:T(8,128)(2,1)S(1)} %copy-done.1, s32[4,8,128]{2,1,0:T(8,128)S(1)} %pad.4.ids, bf16[128,256]{1,0:T(8,128)(2,1)S(1)} %copy-done.3), custom_call_target="tpu_custom_call" | custom-call | tf_op jit(solution)/shard_map/pallas_call | solution.py:578
  110.2 0.7 copy.12
  110.9 0.7 copy.13
  (1 shorter events, 0.0 us)
Async XLA Ops:
  1.3 1.0 copy-start
  2.4 1.0 copy-start.1
  3.4 0.8 copy-start.2
  4.3 0.8 copy-start.3

commit v2 on v1

v2 whole, which is shorter than its diff:
```python
import jax
import jax.numpy as jnp
from jax import lax
from jax.experimental import pallas as pl
from jax.experimental.pallas import tpu as pltpu

P = jax.sharding.PartitionSpec
MESH = pl.DeviceIdType.MESH
f32, bf16, i32 = jnp.float32, jnp.bfloat16, jnp.int32

SHARP = 16.0
EMPTY = 1024.0
PEERS = 32
ROUNDS = 4
GROUP = 4


def iota(shape, dim):
    return lax.broadcasted_iota(i32, shape, dim)


def low_lanes(shape):
    return iota(shape, 1) % 128 < 64


def swap(x):
    return pltpu.roll(x, 64, 1)


def mm(a, b):
    return lax.dot_general(a, b, (((1,), (0,)), ((), ())), preferred_element_type=f32)


def mm_t(a, b):
    return lax.dot_general(a, b, (((1,), (1,)), ((), ())), preferred_element_type=f32)


def split2(x):
    high = x.astype(bf16)
    return high, (x - high.astype(f32)).astype(bf16)


def rank_codes(ids):
    rows = jnp.concatenate([ids[r].astype(f32) for r in range(ROUNDS)], axis=0)
    columns = jnp.concatenate([rows, jnp.zeros((112, 128), f32)], axis=0).T
    before = iota((128, 128), 0) < iota((128, 128), 1)
    codes = []
    for k in range(GROUP):
        code = jnp.zeros((8, 128), f32)
        for r in range(ROUNDS):
            at = 4 * r + k
            same = (columns[:, at : at + 1] == rows[at : at + 1, :]) & before
            rank = jnp.sum(jnp.where(same, 1.0, 0.0), axis=0, keepdims=True)
            code = jnp.where(iota((8, 128), 0) == r, rows[at : at + 1, :] + 128.0 * rank, code)
        codes.append(code.astype(i32))
    return codes


def places(codes):
    bucket, rank = codes & 127, codes >> 7
    block = iota((8, 512), 1) >> 7
    slot = bucket * 4 + block
    both = jnp.concatenate([slot[:4].astype(f32), rank[:4].astype(f32)], axis=0)
    columns = []
    for m in range(GROUP):
        tile = both[:, 128 * m : 128 * m + 128]
        columns.append(jnp.concatenate([tile, jnp.zeros((120, 128), f32)], axis=0).T)
    return bucket, rank, slot, jnp.concatenate(columns, axis=0)


def slot_onehot(slot_row):
    return jnp.where(iota((512, 512), 0) == slot_row, 1.0, 0.0).astype(bf16)


def token_onehot(slot_column):
    return jnp.where(iota((512, 512), 1).astype(f32) == slot_column, 1.0, 0.0).astype(bf16)


def half_mask(rank_column):
    half = (iota((512, 128), 1) >> 6).astype(f32)
    return jnp.where(half == rank_column, 1.0, 0.0).astype(bf16)


def halves(tile):
    top, bottom = tile[:64], tile[64:]
    low = low_lanes((64, 128))
    return jnp.where(low, top, swap(bottom)).astype(bf16), jnp.where(low, swap(top), bottom).astype(bf16)


def pack_cot(onehot, rows, mask):
    out = mm(onehot, jnp.concatenate([rows * mask, mask], axis=1))
    return jnp.where(out[:, 128:256] > 0.5, out[:, 0:128], EMPTY).astype(bf16)


def pack(onehot, rows, mask):
    return mm(onehot, rows * mask).astype(bf16)


def regroup():
    p, c = iota((128, 128), 0), iota((128, 128), 1)
    hit = ((c >> 4) == ((p & 31) >> 2)) & (((c & 15) >> 2) == (p >> 5)) & ((c & 3) == (p & 3))
    return jnp.where(hit, 1.0, 0.0).astype(bf16)


def regroup_back():
    c, p = iota((128, 128), 0), iota((128, 128), 1)
    hit = ((c >> 4) == ((p & 31) >> 2)) & (((c & 15) >> 2) == (p >> 5)) & ((c & 3) == (p & 3))
    return jnp.where(hit, 1.0, 0.0).astype(bf16)


def half_ones():
    r, c = iota((256, 128), 0), iota((256, 128), 1)
    return jnp.where(((r & 127) >> 6) == (c >> 6), 1.0, 0.0).astype(bf16)


def half_sums(x, ones):
    high, low = split2(x)
    return mm(jnp.concatenate([high, low], axis=1), ones)


def on_rows(x):
    return jnp.concatenate([x, swap(x)], axis=0)


def on_rows_low(x):
    low = low_lanes(x.shape)
    return jnp.concatenate([jnp.where(low, x, 0.0), jnp.where(low, swap(x), 0.0)], axis=0)


def on_diagonal(x):
    low, turned = low_lanes(x.shape), swap(x)
    return jnp.concatenate(
        [jnp.where(low, x, 0.0), jnp.where(low, turned, 0.0), jnp.where(low, 0.0, turned), jnp.where(low, 0.0, x)],
        axis=0,
    ).astype(bf16)


def side_by_side(x):
    return jnp.concatenate([x[:128], x[128:]], axis=1)


def diagonal():
    return iota((256, 256), 0) == iota((256, 256), 1)


def owner_scores(shared, cot, ones):
    shared = shared.astype(f32)
    scale = lax.rsqrt(half_sums(shared * shared, ones) + 1e-6)
    unit = shared * scale
    scores = mm_t(on_rows_low(unit).astype(bf16), on_rows(unit).astype(bf16))
    weights = jnp.where(diagonal(), 1.0, jnp.exp(SHARP * scores))
    low = low_lanes((128, 128))
    valid = jnp.where(cot.astype(f32) < 0.5 * EMPTY, 1.0, 0.0)
    turned = swap(valid)
    valid = jnp.concatenate([jnp.where(low, valid, turned), jnp.where(low, turned, valid)], axis=0)
    totals = jnp.sum(weights * jnp.concatenate([valid, valid], axis=1), axis=0, keepdims=True)
    return weights, side_by_side(weights.astype(bf16)), unit, scale, totals


def owner_outputs(weights, beside, values, cot):
    values, cot = values.astype(f32), cot.astype(f32)
    along = mm_t(on_rows_low(values).astype(bf16), on_rows(cot).astype(bf16))
    products = jnp.sum(weights * along, axis=0, keepdims=True)
    return mm(beside, on_diagonal(values)).astype(bf16), products


def owner_values(beside, cot, columns):
    wide = [jnp.broadcast_to(c, (128, 128)) for c in columns]
    grad_round = jnp.where(low_lanes((128, 128)), wide[0], wide[1]) * cot.astype(f32)
    return mm(beside, on_diagonal(grad_round)).astype(bf16), grad_round.astype(bf16)


def owner_shared(weights, unit, scale, values, grad_round, row, columns, ones):
    low = low_lanes((128, 128))
    wide = jnp.concatenate([jnp.broadcast_to(c, (128, 128)) for c in columns], axis=0)
    values, grad_round = values.astype(f32), grad_round.astype(f32)
    values_turned, grad_turned = swap(values), swap(grad_round)
    left = jnp.concatenate([jnp.where(low, grad_round, values_turned), jnp.where(low, grad_turned, values)], axis=0)
    right = jnp.concatenate([jnp.where(low, values, grad_turned), jnp.where(low, values_turned, grad_round)], axis=0)
    inner = mm_t(left.astype(bf16), right.astype(bf16)) - row - jnp.concatenate([wide, wide], axis=1)
    grad = jnp.where(diagonal(), 0.0, weights * inner).astype(bf16)
    grad_unit = SHARP * mm(side_by_side(grad), on_diagonal(unit))
    return ((grad_unit - unit * half_sums(unit * grad_unit, ones)) * scale).astype(bf16)


def own_tile(first, second):
    first, second = first.astype(f32), second.astype(f32)
    low = low_lanes((64, 128))
    return jnp.concatenate([jnp.where(low, first, swap(second)), jnp.where(low, swap(first), second)], axis=0)


def square(x):
    return jnp.concatenate([x, jnp.zeros((128 - x.shape[0], 128), f32)], axis=0)


def place_onehot(bucket_row, block_row):
    return jnp.where(iota((128, 512), 0) == (bucket_row >> 2) * 4 + block_row, 1.0, 0.0).astype(bf16)


def token_scalars(turned, bucket, rank):
    block = iota((1, 512), 1) >> 7
    total, product = jnp.zeros((1, 512), f32), jnp.zeros((1, 512), f32)
    for r in range(ROUNDS):
        onehot = place_onehot(bucket[r : r + 1], block)
        high, low = split2(turned[16 * r : 16 * r + 16])
        picked = mm(jnp.concatenate([high, low], axis=1), jnp.concatenate([onehot, onehot], axis=0))
        hit = iota((8, 512), 0) == rank[r : r + 1] * 4 + (bucket[r : r + 1] & 3)
        total = total + jnp.sum(jnp.where(hit, picked[0:8], 0.0), axis=0, keepdims=True)
        product = product + jnp.sum(jnp.where(hit, picked[8:16], 0.0), axis=0, keepdims=True)
    inverse = 1.0 / total
    return inverse, product * inverse * inverse


def spread_scalars(inverse, along, bucket, rank):
    block = iota((1, 512), 1) >> 7
    out = []
    for r in range(ROUNDS):
        onehot = place_onehot(bucket[r : r + 1], block)
        hit = iota((8, 512), 0) == rank[r : r + 1] * 4 + (bucket[r : r + 1] & 3)
        left = jnp.concatenate([jnp.where(hit, inverse, 0.0), jnp.where(hit, along, 0.0)], axis=0)
        high, low = split2(left)
        both = mm_t(jnp.concatenate([high, low], axis=0), onehot)
        out.append(both[0:16] + both[16:32])
    return square(jnp.concatenate(out, axis=0))


def kernel(
    tok, key_hbm, value_hbm, ids_hbm, cot_hbm, att_out, gin_out,
    gat, kw, vw, ids, cot, row_send, code_send, row_land, code_land,
    onehot, onehot_t, masks, rows_x, slots_out, slots_in, tasks,
    w_keep, beside_keep, unit_keep, scale_keep, round_keep,
    num_task, num_out, num_in, grad_task, grad_out, grad_in,
    z_rows, z_turn, z_out, z_in, q_turn, q_cols, q_out, q_in, acc, part,
    back_send, back_land, rs_send, rs_land,
    ld, s0, r0, s1, r1, s2, r2, sn, rn, sg, rg, s3, r3, s4, r4, s6, r6, s7, r7,
):
    seq, y = lax.axis_index("seq"), lax.axis_index("head")
    z, xc = lax.div(seq, 8), lax.rem(seq, 8)
    zq, zr = lax.div(z, 4), lax.rem(z, 4)
    me = xc * 4 + y
    rows = [lax.rem(y + o, 4) for o in range(4)]

    loads = ((ids_hbm, ids), (cot_hbm, cot), (tok, gat.at[y]), (key_hbm, kw), (value_hbm, vw))
    for i, (src, dst) in enumerate(loads):
        pltpu.make_async_copy(src, dst, ld.at[i]).start()

    def loaded(i):
        pltpu.make_async_copy(loads[i][0], loads[i][1], ld.at[i]).wait()

    def slab(d):
        return (z * 8 + lax.div(d, 4), lax.rem(d, 4))

    def partner(i):
        return ((4 * i + y) * 8 + xc, zr)

    def arrived(ref, sem):
        pltpu.make_async_copy(ref, ref, sem).wait()

    def to_partner(i, src, land, send_sem, recv_sem):
        @pl.when(4 * i + y == z)
        def _():
            pltpu.make_async_copy(src, land.at[zq], recv_sem.at[zq]).start()

        @pl.when(4 * i + y != z)
        def _():
            pltpu.make_async_remote_copy(
                src, land.at[zq], send_sem.at[i], recv_sem.at[zq], device_id=partner(i), device_id_type=MESH
            ).start()

    def partner_sent(i, src, send_sem):
        @pl.when(4 * i + y != z)
        def _():
            arrived(src, send_sem.at[i])

    def to_slab(out_at, in_at, send_sem, recv_sem):
        pltpu.make_async_copy(out_at(me), in_at(me), recv_sem).start()

        def start(column, row):
            d = column * 4 + row
            pltpu.make_async_remote_copy(
                out_at(d), in_at(me), send_sem, recv_sem, device_id=(z * 8 + column, row), device_id_type=MESH
            ).start()

        def send(o, carry):
            column = lax.rem(xc + o, 8)
            for row in rows:
                start(column, row)
            return carry

        for row in rows[1:]:
            start(xc, row)
        lax.fori_loop(1, 8, send, 0)

    barrier = pltpu.get_barrier_semaphore()

    def greet(o, carry):
        pl.semaphore_signal(barrier, 1, device_id=slab(lax.rem(me + o, PEERS)), device_id_type=MESH)
        return carry

    lax.fori_loop(1, PEERS, greet, 0)
    for i in range(GROUP):

        @pl.when(4 * i + y != z)
        def _(i=i):
            pl.semaphore_signal(barrier, 1, device_id=partner(i), device_id_type=MESH)

    loaded(0)
    for k, code in enumerate(rank_codes([ids[r] for r in range(ROUNDS)])):
        code_send[k] = code
    loaded(1)
    low64 = low_lanes((64, 128))
    for k in range(0, GROUP, 2):
        row_send[2, k], row_send[2, k + 1] = halves(cot[:, 64 * k : 64 * k + 128].astype(f32))

    pl.semaphore_wait(barrier, jnp.where(zr == y, 34, 35))

    for k in range(GROUP):
        to_partner(k, code_send.at[k], code_land, s1.at[0], r1.at[0])
    for o in range(1, 4):
        pltpu.make_async_remote_copy(
            tok, gat.at[y], s0.at[o - 1], r0.at[o - 1], device_id=(seq, lax.rem(y + o, 4)), device_id_type=MESH
        ).start()
    for k in range(GROUP):
        to_partner(k, row_send.at[2, k], row_land.at[2], s1.at[3], r1.at[3])

    for m in range(GROUP):
        arrived(code_land.at[m], r1.at[0, m])
    codes = jnp.concatenate([code_land[m] for m in range(GROUP)], axis=1)
    bucket, rank, slot, columns = places(codes)
    for r in range(ROUNDS):
        onehot[r] = slot_onehot(slot[r : r + 1])
        masks[r] = half_mask(columns[:, 4 + r : 5 + r])

    def piece(d):
        return pl.ds(pl.multiple_of(d * 16, 16), 16)

    def spread(a):
        for m in range(GROUP):
            arrived(row_land.at[a, m], r1.at[a + 1, m])
            landed = row_land[a, m].astype(f32)
            turned = swap(landed)
            rows_x[a, 128 * m : 128 * m + 64, :] = jnp.where(low64, landed, turned).astype(bf16)
            rows_x[a, 128 * m + 64 : 128 * m + 128, :] = jnp.where(low64, turned, landed).astype(bf16)

    spread(2)

    def pack_cots(r, carry):
        slots_out[2, r] = pack_cot(onehot[r], rows_x[2], masks[r])
        return carry

    lax.fori_loop(0, ROUNDS, pack_cots, 0)
    to_slab(lambda d: slots_out.at[2, :, piece(d), :], lambda d: slots_in.at[2, :, piece(d), :], s2.at[3], r2.at[3])

    for i in (2, 3, 4):
        loaded(i)
    for a, weight in enumerate((kw, vw)):
        result = mm(gat[y], weight[pl.ds(pl.multiple_of(y * 256, 256), 256), :])
        for o in range(1, 4):
            source = lax.rem(y + 4 - o, 4)
            if a == 0:
                arrived(gat.at[source], r0.at[o - 1])
            result = result + mm(gat[source], weight[pl.ds(pl.multiple_of(source * 256, 256), 256), :])
        for k in range(0, GROUP, 2):
            row_send[a, k], row_send[a, k + 1] = halves(result[:, 64 * k : 64 * k + 128])
        for k in range(GROUP):
            to_partner(k, row_send.at[a, k], row_land.at[a], s1.at[a + 1], r1.at[a + 1])

    spread(0)

    def pack_shared(r, carry):
        slots_out[0, r] = pack(onehot[r], rows_x[0], masks[r])
        return carry

    lax.fori_loop(0, ROUNDS, pack_shared, 0)
    to_slab(lambda d: slots_out.at[0, :, piece(d), :], lambda d: slots_in.at[0, :, piece(d), :], s2.at[0], r2.at[0])
    spread(1)

    def pack_values(p, carry):
        for i in range(2):
            slots_out[1, 2 * p + i] = pack(onehot[2 * p + i], rows_x[1], masks[2 * p + i])
        two = pl.ds(2 * p, 2)
        to_slab(
            lambda d: slots_out.at[1, two, piece(d), :],
            lambda d: slots_in.at[1, two, piece(d), :],
            s2.at[p + 1],
            r2.at[p + 1],
        )
        return carry

    lax.fori_loop(0, 2, pack_values, 0)

    for r in range(ROUNDS):
        onehot_t[r] = token_onehot(columns[:, r : r + 1])

    ones = half_ones()
    sort, unsort = regroup(), regroup_back()
    z_rows[...] = jnp.zeros((128, 128), f32)

    def sort_rows(a, r):
        for g in range(4):
            moved = mm(sort, slots_in[a, r, 128 * g : 128 * g + 128, :]).astype(bf16)
            for b in range(GROUP):
                tasks[r * 4 + b, a, 32 * g : 32 * g + 32, :] = moved[32 * b : 32 * b + 32]

    def sort_cots(r, carry):
        sort_rows(2, r)
        return carry

    arrived(slots_in.at[2], r2.at[3])
    lax.fori_loop(0, ROUNDS, sort_cots, 0)

    def scores_round(r, carry):
        sort_rows(0, r)
        for b in range(GROUP):
            t = r * 4 + b
            weights, beside, unit, scale, totals = owner_scores(tasks[t, 0], tasks[t, 2], ones)
            w_keep[t] = weights
            beside_keep[t] = beside
            unit_keep[t] = unit
            scale_keep[t] = scale
            line = r * 16 + b
            z_rows[pl.ds(line, 1), :] = totals[:, :128]
            z_rows[pl.ds(line + 4, 1), :] = totals[:, 128:]
        return carry

    arrived(slots_in.at[0], r2.at[0])
    lax.fori_loop(0, ROUNDS, scores_round, 0)

    def outputs_round(r):
        sort_rows(1, r)
        for b in range(GROUP):
            t = r * 4 + b
            numerator, products = owner_outputs(w_keep[t], beside_keep[t], tasks[t, 1], tasks[t, 2])
            num_task[b] = numerator
            line = r * 16 + b
            z_rows[pl.ds(line + 8, 1), :] = products[:, :128]
            z_rows[pl.ds(line + 12, 1), :] = products[:, 128:]
        for g in range(4):
            moved = jnp.concatenate([num_task[b, 32 * g : 32 * g + 32, :] for b in range(GROUP)], axis=0)
            num_out[r, 128 * g : 128 * g + 128, :] = mm(unsort, moved).astype(bf16)

    def outputs_pair(p, carry):
        arrived(slots_in.at[1, pl.ds(2 * p, 2)], r2.at[p + 1])
        for i in range(2):
            outputs_round(2 * p + i)
        return carry

    lax.fori_loop(0, 2, outputs_pair, 0)

    def send_numerators(p):
        two = pl.ds(2 * p, 2)
        to_slab(lambda d: num_out.at[two, piece(d), :], lambda d: num_in.at[two, piece(d), :], sn.at[p], rn.at[p])

    z_turn[...] = z_rows[...].T
    for d in range(PEERS):
        z_out[d] = z_turn[4 * d : 4 * d + 4, :]
    to_slab(lambda d: z_out.at[d], lambda d: z_in.at[d], s3.at[0], r3.at[0])
    send_numerators(0)
    arrived(z_in, r3.at[0])
    for d in range(PEERS):
        q_turn[4 * d : 4 * d + 4, :] = z_in[d]
    inverse, along = token_scalars(q_turn[...].T, bucket, rank)
    z_turn[...] = spread_scalars(inverse, along, bucket, rank).T
    for d in range(PEERS):
        q_out[d] = z_turn[4 * d : 4 * d + 4, :]
    to_slab(lambda d: q_out.at[d], lambda d: q_in.at[d], s4.at[0], r4.at[0])
    send_numerators(1)

    arrived(q_in, r4.at[0])
    for d in range(PEERS):
        q_cols[4 * d : 4 * d + 4, :] = q_in[d]
    q_turn[...] = q_cols[...].T

    def nearby(line):
        return pltpu.roll(q_cols[...], lax.rem(128 - line, 128), 1)

    def unsort_grads(a, r):
        for g in range(4):
            moved = jnp.concatenate([grad_task[b, 32 * g : 32 * g + 32, :] for b in range(GROUP)], axis=0)
            grad_out[a, r, 128 * g : 128 * g + 128, :] = mm(unsort, moved).astype(bf16)

    def values_pair(p, carry):
        for i in range(2):
            r = 2 * p + i
            for b in range(GROUP):
                t = r * 4 + b
                near = nearby(r * 16 + b)
                grad_values, grad_round = owner_values(beside_keep[t], tasks[t, 2], [near[:, c : c + 1] for c in (0, 4)])
                round_keep[t] = grad_round
                grad_task[b] = grad_values
            unsort_grads(0, r)
        two = pl.ds(2 * p, 2)
        to_slab(
            lambda d: grad_out.at[0, two, piece(d), :], lambda d: grad_in.at[0, two, piece(d), :], sg.at[p], rg.at[p]
        )
        return carry

    lax.fori_loop(0, 2, values_pair, 0)

    def shared_round(r, carry):
        for b in range(GROUP):
            t = r * 4 + b
            line = r * 16 + b
            near = nearby(line)
            row = jnp.concatenate([q_turn[pl.ds(line + 8, 1), :], q_turn[pl.ds(line + 12, 1), :]], axis=1)
            grad_task[b] = owner_shared(
                w_keep[t], unit_keep[t], scale_keep[t], tasks[t, 1], round_keep[t], row,
                [near[:, c : c + 1] for c in (8, 12)], ones,
            )
        unsort_grads(1, r)
        to_slab(
            lambda d: grad_out.at[1, r, piece(d), :], lambda d: grad_in.at[1, r, piece(d), :], sg.at[r + 2], rg.at[r + 2]
        )
        return carry

    lax.fori_loop(0, ROUNDS, shared_round, 0)

    def add(source, r):
        acc[...] += mm(onehot_t[r], source[r]) * masks[r].astype(f32)

    def summed(source, sems):
        acc[...] = jnp.zeros((512, 128), f32)

        def pair(p, carry):
            arrived(source.at[pl.ds(2 * p, 2)], sems.at[p])
            for i in range(2):
                add(source, 2 * p + i)
            return carry

        lax.fori_loop(0, 2, pair, 0)

    def send_back(a, scale):
        for m in range(GROUP):
            rows = acc[128 * m : 128 * m + 128, :]
            rows = rows + swap(rows)
            if scale is not None:
                rows = rows * jnp.broadcast_to(scale[:, 128 * m : 128 * m + 128], (128, 128)).T
            back_send[a, m] = jnp.where(low64, rows[:64], rows[64:]).astype(bf16)
            to_partner(m, back_send.at[a, m], back_land.at[a], s6.at[a], r6.at[a])

    def own_rows(a):
        for k in range(GROUP):
            arrived(back_land.at[a, k], r6.at[a, k])
        return [own_tile(back_land[a, k], back_land[a, k + 1]) for k in range(0, GROUP, 2)]

    summed(num_in, rn)
    send_back(0, inverse)
    summed(grad_in.at[0], rg)
    send_back(1, None)
    for k, tile in enumerate(own_rows(0)):
        att_out[:, 128 * k : 128 * k + 128] = tile
    acc[...] = jnp.zeros((512, 128), f32)

    def add_shared(r, carry):
        arrived(grad_in.at[1, r], rg.at[r + 2])
        add(grad_in.at[1], r)
        return carry

    lax.fori_loop(0, ROUNDS, add_shared, 0)
    send_back(2, None)

    left = jnp.concatenate(own_rows(1), axis=1).astype(bf16)
    for o in range(4):
        part[o] = mm_t(left, vw[pl.ds(pl.multiple_of(lax.rem(y + o, 4) * 256, 256), 256), :])
    left = jnp.concatenate(own_rows(2), axis=1).astype(bf16)
    for o in range(1, 4):
        d = lax.rem(y + o, 4)
        rs_send[o - 1] = (part[o] + mm_t(left, kw[pl.ds(pl.multiple_of(d * 256, 256), 256), :])).astype(bf16)
        pltpu.make_async_remote_copy(
            rs_send.at[o - 1], rs_land.at[o - 1], s7.at[o - 1], r7.at[o - 1], device_id=(seq, d), device_id_type=MESH
        ).start()
    total = part[0] + mm_t(left, kw[pl.ds(pl.multiple_of(y * 256, 256), 256), :])
    for o in range(1, 4):
        arrived(rs_land.at[o - 1], r7.at[o - 1])
        total = total + rs_land[o - 1].astype(f32)
    gin_out[...] = total

    for o in range(3):
        arrived(gat.at[o], s0.at[o])
        arrived(rs_send.at[o], s7.at[o])
    for k in range(GROUP):
        partner_sent(k, code_send.at[k], s1.at[0])
        for a in range(3):
            partner_sent(k, row_send.at[a, k], s1.at[a + 1])
            partner_sent(k, back_send.at[a, k], s6.at[a])
    rest = pl.ds(0, 16 * (PEERS - 1))
    arrived(slots_out.at[0, :, rest, :], s2.at[0])
    arrived(slots_out.at[2, :, rest, :], s2.at[3])
    for p in range(2):
        two = pl.ds(2 * p, 2)
        arrived(slots_out.at[1, two, rest, :], s2.at[p + 1])
        arrived(num_out.at[two, rest, :], sn.at[p])
        arrived(grad_out.at[0, two, rest, :], sg.at[p])
    for r in range(ROUNDS):
        arrived(grad_out.at[1, r, rest, :], sg.at[r + 2])
    arrived(z_out.at[pl.ds(0, PEERS - 1)], s3.at[0])
    arrived(q_out.at[pl.ds(0, PEERS - 1)], s4.at[0])


def shards(tokens, key_weight, value_weight, buckets, cotangent):
    vmem, hbm = pl.BlockSpec(memory_space=pltpu.VMEM), pl.BlockSpec(memory_space=pl.ANY)
    v, dma = pltpu.VMEM, pltpu.SemaphoreType.DMA
    scratch = [
        v((4, 128, 256), bf16),
        v((1024, 256), bf16),
        v((1024, 256), bf16),
        v((4, 4, 128), i32),
        v((128, 256), bf16),
        v((3, 4, 64, 128), bf16),
        v((4, 8, 128), i32),
        v((3, 4, 64, 128), bf16),
        v((4, 8, 128), i32),
        v((4, 512, 512), bf16),
        v((4, 512, 512), bf16),
        v((4, 512, 128), bf16),
        v((3, 512, 128), bf16),
        v((3, 4, 512, 128), bf16),
        v((3, 4, 512, 128), bf16),
        v((16, 3, 128, 128), bf16),
        v((16, 256, 256), f32),
        v((16, 128, 512), bf16),
        v((16, 128, 128), f32),
        v((16, 128, 128), f32),
        v((16, 128, 128), bf16),
        v((4, 128, 128), bf16),
        v((4, 512, 128), bf16),
        v((4, 512, 128), bf16),
        v((4, 128, 128), bf16),
        v((2, 4, 512, 128), bf16),
        v((2, 4, 512, 128), bf16),
        v((128, 128), f32),
        v((128, 128), f32),
        v((32, 4, 128), f32),
        v((32, 4, 128), f32),
        v((128, 128), f32),
        v((128, 128), f32),
        v((32, 4, 128), f32),
        v((32, 4, 128), f32),
        v((512, 128), f32),
        v((4, 128, 256), f32),
        v((3, 4, 64, 128), bf16),
        v((3, 4, 64, 128), bf16),
        v((3, 128, 256), bf16),
        v((3, 128, 256), bf16),
        dma((5,)),
        dma((3,)), dma((3,)),
        dma((4, 4)), dma((4, 4)),
        dma((4,)), dma((4,)),
        dma((2,)), dma((2,)),
        dma((6,)), dma((6,)),
        dma((1,)), dma((1,)),
        dma((1,)), dma((1,)),
        dma((3, 4)), dma((3, 4)),
        dma((3,)), dma((3,)),
    ]
    return pl.pallas_call(
        kernel,
        out_shape=(jax.ShapeDtypeStruct((128, 256), f32), jax.ShapeDtypeStruct((128, 256), f32)),
        in_specs=[hbm] * 5,
        out_specs=(vmem, vmem),
        scratch_shapes=scratch,
        compiler_params=pltpu.CompilerParams(
            collective_id=0, has_side_effects=True, vmem_limit_bytes=60 * 1024 * 1024
        ),
    )(tokens, key_weight, value_weight, buckets[..., 0], cotangent)


def solution(mesh):
    in_specs = (
        P("seq", "head"),
        P(None, "head"),
        P(None, "head"),
        P(None, "head", "seq", None),
        P("seq", "head"),
    )
    out_specs = (P("seq", "head"), P("seq", "head"))
    return jax.shard_map(shards, mesh=mesh, in_specs=in_specs, out_specs=out_specs, check_vma=False)
```

time: 114 us -> 108 us (0.947)
  local copies, waits for them, and re-layouts: 5.78 us -> 2.26 us
  Pallas kernels: 105 us -> 103 us
    unnamed x11 -> x4, local copies, waits for them, and re-layouts: 5.77 us -> 2.26 us
    pallas_call x1, Pallas kernels: 105 us -> 103 us  [shards(): pl.pallas_call(kernel, out_shape=(jax.ShapeDtypeStruct((128, 256), f32),...]
where the time goes in v2:
time: 108 us; the launch traced here: 106 us
  Pallas kernels  103 us (95%)
  local copies, waits for them, and re-layouts  2.26 us (2%)
    pallas_call x1, Pallas kernels, shards(): pl.pallas_call(kernel, out_shape=(jax.ShapeDtypeStruct((128, 256), f32),...  103 us
    unnamed x4, local copies, waits for them, and re-layouts  2.26 us

profile of v2, /device:TPU:6, one launch (start us, length us, event | category | flops | bytes accessed | tf_op | source)
XLA Modules:
  0.0 106.4 jit_solution(16497666350321949920)
XLA Ops:
  0.6 103.5 %shard_map.68 = (f32[128,256]{1,0:T(8,128)}, f32[128,256]{1,0:T(8,128)}) custom-call(bf16[128,256]{1,0:T(8,128)(2,1)} %tok.1, bf16[1024,256]{1,0:T(8,128)(2,1)} %key_hbm.1, bf16[1024,256]{1,0:T(8,128)(2,1)} %value_hbm.1, s32[4,4,128]{2,1,0:T(4,128)} %bitcast.1, bf16[128,256]{1,0:T(8,128)(2,1)} %cot_hbm.1), custom_call_target="tpu_custom_call" | custom-call | tf_op jit(solution)/shard_map/pallas_call | solution.py:656
  104.1 0.0 copy-start
  104.1 1.6 %copy.9 = f32[128,256]{1,0:T(8,128)} copy(f32[128,256]{1,0:T(8,128)} %get-tuple-element.4) | data formatting | bytes 262144
  105.7 0.0 copy-done
  105.7 0.7 copy.10
Async XLA Ops:
  104.1 1.6 %copy-start = (f32[128,256]{1,0:T(8,128)S(1)}, f32[128,256]{1,0:T(8,128)}, u32[]{:S(2)}) copy-start(f32[128,256]{1,0:T(8,128)} %get-tuple-element.5) | copy-start | bytes 393220

commit v3 on v2

--- a/solution.py
+++ b/solution.py
@@ -250,25 +250,39 @@
     def slab(d):
         return (z * 8 + lax.div(d, 4), lax.rem(d, 4))
 
-    def partner(i):
-        return ((4 * i + y) * 8 + xc, zr)
+    first = z < 4
+    turn = jnp.where(first, 0, lax.rem(z + 2, 3) + 1)
+    block = jnp.where(first, z, lax.div(z + 2, 3) - 2)
+    alone = first & (z == y)
+
+    def head_place(i):
+        return ((4 * i + y) * 8 + xc, lax.rem(turn + y, 4))
+
+    def block_home(i):
+        back = lax.rem(y + 4 - zr, 4)
+        return (jnp.where(back == 0, i, 3 + 3 * i + back) * 8 + xc, zr)
 
     def arrived(ref, sem):
         pltpu.make_async_copy(ref, ref, sem).wait()
 
-    def to_partner(i, src, land, send_sem, recv_sem):
-        @pl.when(4 * i + y == z)
+    to_head = (head_place, block, lambda i: alone & (zq == i))
+    to_home = (block_home, zq, lambda i: alone & (zr == i))
+
+    def to_partner(way, i, src, land, send_sem, recv_sem):
+        partner, slot, itself = way
+
+        @pl.when(itself(i))
         def _():
-            pltpu.make_async_copy(src, land.at[zq], recv_sem.at[zq]).start()
-
-        @pl.when(4 * i + y != z)
+            pltpu.make_async_copy(src, land.at[slot], recv_sem.at[slot]).start()
+
+        @pl.when(jnp.logical_not(itself(i)))
         def _():
             pltpu.make_async_remote_copy(
-                src, land.at[zq], send_sem.at[i], recv_sem.at[zq], device_id=partner(i), device_id_type=MESH
+                src, land.at[slot], send_sem.at[i], recv_sem.at[slot], device_id=partner(i), device_id_type=MESH
             ).start()
 
-    def partner_sent(i, src, send_sem):
-        @pl.when(4 * i + y != z)
+    def partner_sent(way, i, src, send_sem):
+        @pl.when(jnp.logical_not(way[2](i)))
         def _():
             arrived(src, send_sem.at[i])
 
@@ -300,9 +314,11 @@
     lax.fori_loop(1, PEERS, greet, 0)
     for i in range(GROUP):
 
-        @pl.when(4 * i + y != z)
-        def _(i=i):
-            pl.semaphore_signal(barrier, 1, device_id=partner(i), device_id_type=MESH)
+        for way in (to_head, to_home):
+
+            @pl.when(jnp.logical_not(way[2](i)))
+            def _(i=i, way=way):
+                pl.semaphore_signal(barrier, 1, device_id=way[0](i), device_id_type=MESH)
 
     loaded(0)
     for k, code in enumerate(rank_codes([ids[r] for r in range(ROUNDS)])):
@@ -312,16 +328,16 @@
     for k in range(0, GROUP, 2):
         row_send[2, k], row_send[2, k + 1] = halves(cot[:, 64 * k : 64 * k + 128].astype(f32))
 
-    pl.semaphore_wait(barrier, jnp.where(zr == y, 34, 35))
+    pl.semaphore_wait(barrier, jnp.where(alone, 37, 39))
 
     for k in range(GROUP):
-        to_partner(k, code_send.at[k], code_land, s1.at[0], r1.at[0])
+        to_partner(to_head, k, code_send.at[k], code_land, s1.at[0], r1.at[0])
     for o in range(1, 4):
         pltpu.make_async_remote_copy(
             tok, gat.at[y], s0.at[o - 1], r0.at[o - 1], device_id=(seq, lax.rem(y + o, 4)), device_id_type=MESH
         ).start()
     for k in range(GROUP):
-        to_partner(k, row_send.at[2, k], row_land.at[2], s1.at[3], r1.at[3])
+        to_partner(to_head, k, row_send.at[2, k], row_land.at[2], s1.at[3], r1.at[3])
 
     for m in range(GROUP):
         arrived(code_land.at[m], r1.at[0, m])
@@ -341,15 +357,6 @@
             turned = swap(landed)
             rows_x[a, 128 * m : 128 * m + 64, :] = jnp.where(low64, landed, turned).astype(bf16)
             rows_x[a, 128 * m + 64 : 128 * m + 128, :] = jnp.where(low64, turned, landed).astype(bf16)
-
-    spread(2)
-
-    def pack_cots(r, carry):
-        slots_out[2, r] = pack_cot(onehot[r], rows_x[2], masks[r])
-        return carry
-
-    lax.fori_loop(0, ROUNDS, pack_cots, 0)
-    to_slab(lambda d: slots_out.at[2, :, piece(d), :], lambda d: slots_in.at[2, :, piece(d), :], s2.at[3], r2.at[3])
 
     for i in (2, 3, 4):
         loaded(i)
@@ -363,7 +370,16 @@
         for k in range(0, GROUP, 2):
             row_send[a, k], row_send[a, k + 1] = halves(result[:, 64 * k : 64 * k + 128])
         for k in range(GROUP):
-            to_partner(k, row_send.at[a, k], row_land.at[a], s1.at[a + 1], r1.at[a + 1])
+            to_partner(to_head, k, row_send.at[a, k], row_land.at[a], s1.at[a + 1], r1.at[a + 1])
+
+    spread(2)
+
+    def pack_cots(r, carry):
+        slots_out[2, r] = pack_cot(onehot[r], rows_x[2], masks[r])
+        return carry
+
+    lax.fori_loop(0, ROUNDS, pack_cots, 0)
+    to_slab(lambda d: slots_out.at[2, :, piece(d), :], lambda d: slots_in.at[2, :, piece(d), :], s2.at[3], r2.at[3])
 
     spread(0)
 
@@ -466,6 +482,34 @@
     to_slab(lambda d: q_out.at[d], lambda d: q_in.at[d], s4.at[0], r4.at[0])
     send_numerators(1)
 
+    def add(source, r):
+        acc[...] += mm(onehot_t[r], source[r]) * masks[r].astype(f32)
+
+    def summed(source, sems):
+        acc[...] = jnp.zeros((512, 128), f32)
+
+        def pair(p, carry):
+            arrived(source.at[pl.ds(2 * p, 2)], sems.at[p])
+            for i in range(2):
+                add(source, 2 * p + i)
+            return carry
+
+        lax.fori_loop(0, 2, pair, 0)
+
+    def send_back(a, scale):
+        for m in range(GROUP):
+            rows = acc[128 * m : 128 * m + 128, :]
+            rows = rows + swap(rows)
+            if scale is not None:
+                rows = rows * jnp.broadcast_to(scale[:, 128 * m : 128 * m + 128], (128, 128)).T
+            back_send[a, m] = jnp.where(low64, rows[:64], rows[64:]).astype(bf16)
+            to_partner(to_home, m, back_send.at[a, m], back_land.at[a], s6.at[a], r6.at[a])
+
+    def own_rows(a):
+        for k in range(GROUP):
+            arrived(back_land.at[a, k], r6.at[a, k])
+        return [own_tile(back_land[a, k], back_land[a, k + 1]) for k in range(0, GROUP, 2)]
+
     arrived(q_in, r4.at[0])
     for d in range(PEERS):
         q_cols[4 * d : 4 * d + 4, :] = q_in[d]
@@ -496,6 +540,8 @@
         return carry
 
     lax.fori_loop(0, 2, values_pair, 0)
+    summed(num_in, rn)
+    send_back(0, inverse)
 
     def shared_round(r, carry):
         for b in range(GROUP):
@@ -515,40 +561,8 @@
 
     lax.fori_loop(0, ROUNDS, shared_round, 0)
 
-    def add(source, r):
-        acc[...] += mm(onehot_t[r], source[r]) * masks[r].astype(f32)
-
-    def summed(source, sems):
-        acc[...] = jnp.zeros((512, 128), f32)
-
-        def pair(p, carry):
-            arrived(source.at[pl.ds(2 * p, 2)], sems.at[p])
-            for i in range(2):
-                add(source, 2 * p + i)
-            return carry
-
-        lax.fori_loop(0, 2, pair, 0)
-
-    def send_back(a, scale):
-        for m in range(GROUP):
-            rows = acc[128 * m : 128 * m + 128, :]
-            rows = rows + swap(rows)
-            if scale is not None:
-                rows = rows * jnp.broadcast_to(scale[:, 128 * m : 128 * m + 128], (128, 128)).T
-            back_send[a, m] = jnp.where(low64, rows[:64], rows[64:]).astype(bf16)
-            to_partner(m, back_send.at[a, m], back_land.at[a], s6.at[a], r6.at[a])
-
-    def own_rows(a):
-        for k in range(GROUP):
-            arrived(back_land.at[a, k], r6.at[a, k])
-        return [own_tile(back_land[a, k], back_land[a, k + 1]) for k in range(0, GROUP, 2)]
-
-    summed(num_in, rn)
-    send_back(0, inverse)
     summed(grad_in.at[0], rg)
     send_back(1, None)
-    for k, tile in enumerate(own_rows(0)):
-        att_out[:, 128 * k : 128 * k + 128] = tile
     acc[...] = jnp.zeros((512, 128), f32)
 
     def add_shared(r, carry):
@@ -558,6 +572,8 @@
 
     lax.fori_loop(0, ROUNDS, add_shared, 0)
     send_back(2, None)
+    for k, tile in enumerate(own_rows(0)):
+        att_out[:, 128 * k : 128 * k + 128] = tile
 
     left = jnp.concatenate(own_rows(1), axis=1).astype(bf16)
     for o in range(4):
@@ -579,10 +595,10 @@
         arrived(gat.at[o], s0.at[o])
         arrived(rs_send.at[o], s7.at[o])
     for k in range(GROUP):
-        partner_sent(k, code_send.at[k], s1.at[0])
+        partner_sent(to_head, k, code_send.at[k], s1.at[0])
         for a in range(3):
-            partner_sent(k, row_send.at[a, k], s1.at[a + 1])
-            partner_sent(k, back_send.at[a, k], s6.at[a])
+            partner_sent(to_head, k, row_send.at[a, k], s1.at[a + 1])
+            partner_sent(to_home, k, back_send.at[a, k], s6.at[a])
     rest = pl.ds(0, 16 * (PEERS - 1))
     arrived(slots_out.at[0, :, rest, :], s2.at[0])
     arrived(slots_out.at[2, :, rest, :], s2.at[3])

time: 108 us -> 104 us (0.963)
  Pallas kernels: 103 us -> 99.4 us
    pallas_call x1, Pallas kernels: 103 us -> 99.4 us  [shards(): pl.pallas_call(kernel, out_shape=(jax.ShapeDtypeStruct((128, 256), f32),...]
where the time goes in v3:
time: 104 us; the launch traced here: 102 us
  Pallas kernels  99.4 us (96%)
  local copies, waits for them, and re-layouts  2.26 us (2%)
    pallas_call x1, Pallas kernels, shards(): pl.pallas_call(kernel, out_shape=(jax.ShapeDtypeStruct((128, 256), f32),...  99.4 us
    unnamed x4, local copies, waits for them, and re-layouts  2.26 us

profile of v3, /device:TPU:6, one launch (start us, length us, event | category | flops | bytes accessed | tf_op | source)
XLA Modules:
  0.0 102.3 jit_solution(6404655124762773591)
XLA Ops:
  0.6 99.4 %shard_map.68 = (f32[128,256]{1,0:T(8,128)}, f32[128,256]{1,0:T(8,128)}) custom-call(bf16[128,256]{1,0:T(8,128)(2,1)} %tok.1, bf16[1024,256]{1,0:T(8,128)(2,1)} %key_hbm.1, bf16[1024,256]{1,0:T(8,128)(2,1)} %value_hbm.1, s32[4,4,128]{2,1,0:T(4,128)} %bitcast.1, bf16[128,256]{1,0:T(8,128)(2,1)} %cot_hbm.1), custom_call_target="tpu_custom_call" | custom-call | tf_op jit(solution)/shard_map/pallas_call | solution.py:672
  100.0 0.0 copy-start
  100.0 1.6 %copy.9 = f32[128,256]{1,0:T(8,128)} copy(f32[128,256]{1,0:T(8,128)} %get-tuple-element.4) | data formatting | bytes 262144
  101.6 0.0 copy-done
  101.6 0.7 copy.10
Async XLA Ops:
  100.0 1.6 %copy-start = (f32[128,256]{1,0:T(8,128)S(1)}, f32[128,256]{1,0:T(8,128)}, u32[]{:S(2)}) copy-start(f32[128,256]{1,0:T(8,128)} %get-tuple-element.5) | copy-start | bytes 393220

commit v4 on v3

--- a/solution.py
+++ b/solution.py
@@ -339,25 +339,6 @@
     for k in range(GROUP):
         to_partner(to_head, k, row_send.at[2, k], row_land.at[2], s1.at[3], r1.at[3])
 
-    for m in range(GROUP):
-        arrived(code_land.at[m], r1.at[0, m])
-    codes = jnp.concatenate([code_land[m] for m in range(GROUP)], axis=1)
-    bucket, rank, slot, columns = places(codes)
-    for r in range(ROUNDS):
-        onehot[r] = slot_onehot(slot[r : r + 1])
-        masks[r] = half_mask(columns[:, 4 + r : 5 + r])
-
-    def piece(d):
-        return pl.ds(pl.multiple_of(d * 16, 16), 16)
-
-    def spread(a):
-        for m in range(GROUP):
-            arrived(row_land.at[a, m], r1.at[a + 1, m])
-            landed = row_land[a, m].astype(f32)
-            turned = swap(landed)
-            rows_x[a, 128 * m : 128 * m + 64, :] = jnp.where(low64, landed, turned).astype(bf16)
-            rows_x[a, 128 * m + 64 : 128 * m + 128, :] = jnp.where(low64, turned, landed).astype(bf16)
-
     for i in (2, 3, 4):
         loaded(i)
     for a, weight in enumerate((kw, vw)):
@@ -371,6 +352,25 @@
             row_send[a, k], row_send[a, k + 1] = halves(result[:, 64 * k : 64 * k + 128])
         for k in range(GROUP):
             to_partner(to_head, k, row_send.at[a, k], row_land.at[a], s1.at[a + 1], r1.at[a + 1])
+
+    for m in range(GROUP):
+        arrived(code_land.at[m], r1.at[0, m])
+    codes = jnp.concatenate([code_land[m] for m in range(GROUP)], axis=1)
+    bucket, rank, slot, columns = places(codes)
+    for r in range(ROUNDS):
+        onehot[r] = slot_onehot(slot[r : r + 1])
+        masks[r] = half_mask(columns[:, 4 + r : 5 + r])
+
+    def piece(d):
+        return pl.ds(pl.multiple_of(d * 16, 16), 16)
+
+    def spread(a):
+        for m in range(GROUP):
+            arrived(row_land.at[a, m], r1.at[a + 1, m])
+            landed = row_land[a, m].astype(f32)
+            turned = swap(landed)
+            rows_x[a, 128 * m : 128 * m + 64, :] = jnp.where(low64, landed, turned).astype(bf16)
+            rows_x[a, 128 * m + 64 : 128 * m + 128, :] = jnp.where(low64, turned, landed).astype(bf16)
 
     spread(2)
 

time: 104 us -> 102 us (0.981); the launches traced: 102 us -> 101 us
  no operation moved by 1% of the time
where the time goes in v4:
time: 102 us; the launch traced here: 101 us
  Pallas kernels  98.4 us (96%)
  local copies, waits for them, and re-layouts  2.26 us (2%)
    pallas_call x1, Pallas kernels, shards(): pl.pallas_call(kernel, out_shape=(jax.ShapeDtypeStruct((128, 256), f32),...  98.4 us
    unnamed x4, local copies, waits for them, and re-layouts  2.26 us

profile of v4, /device:TPU:6, one launch (start us, length us, event | category | flops | bytes accessed | tf_op | source)
XLA Modules:
  0.0 101.4 jit_solution(14377850058633765942)
XLA Ops:
  0.6 98.4 %shard_map.68 = (f32[128,256]{1,0:T(8,128)}, f32[128,256]{1,0:T(8,128)}) custom-call(bf16[128,256]{1,0:T(8,128)(2,1)} %tok.1, bf16[1024,256]{1,0:T(8,128)(2,1)} %key_hbm.1, bf16[1024,256]{1,0:T(8,128)(2,1)} %value_hbm.1, s32[4,4,128]{2,1,0:T(4,128)} %bitcast.1, bf16[128,256]{1,0:T(8,128)(2,1)} %cot_hbm.1), custom_call_target="tpu_custom_call" | custom-call | tf_op jit(solution)/shard_map/pallas_call | solution.py:672
  99.1 0.0 copy-start
  99.1 1.6 %copy.9 = f32[128,256]{1,0:T(8,128)} copy(f32[128,256]{1,0:T(8,128)} %get-tuple-element.4) | data formatting | bytes 262144
  100.7 0.0 copy-done
  100.7 0.7 copy.10
Async XLA Ops:
  99.1 1.6 %copy-start = (f32[128,256]{1,0:T(8,128)S(1)}, f32[128,256]{1,0:T(8,128)}, u32[]{:S(2)}) copy-start(f32[128,256]{1,0:T(8,128)} %get-tuple-element.5) | copy-start | bytes 393220

commit v5 on v4

--- a/solution.py
+++ b/solution.py
@@ -379,31 +379,28 @@
         return carry
 
     lax.fori_loop(0, ROUNDS, pack_cots, 0)
-    to_slab(lambda d: slots_out.at[2, :, piece(d), :], lambda d: slots_in.at[2, :, piece(d), :], s2.at[3], r2.at[3])
+    to_slab(lambda d: slots_out.at[2, :, piece(d), :], lambda d: slots_in.at[2, :, piece(d), :], s2.at[4], r2.at[4])
 
     spread(0)
 
-    def pack_shared(r, carry):
-        slots_out[0, r] = pack(onehot[r], rows_x[0], masks[r])
-        return carry
-
-    lax.fori_loop(0, ROUNDS, pack_shared, 0)
-    to_slab(lambda d: slots_out.at[0, :, piece(d), :], lambda d: slots_in.at[0, :, piece(d), :], s2.at[0], r2.at[0])
+    def pack_pair(a):
+        def pair(p, carry):
+            for i in range(2):
+                slots_out[a, 2 * p + i] = pack(onehot[2 * p + i], rows_x[a], masks[2 * p + i])
+            two = pl.ds(2 * p, 2)
+            to_slab(
+                lambda d: slots_out.at[a, two, piece(d), :],
+                lambda d: slots_in.at[a, two, piece(d), :],
+                s2.at[2 * a + p],
+                r2.at[2 * a + p],
+            )
+            return carry
+
+        return pair
+
+    lax.fori_loop(0, 2, pack_pair(0), 0)
     spread(1)
-
-    def pack_values(p, carry):
-        for i in range(2):
-            slots_out[1, 2 * p + i] = pack(onehot[2 * p + i], rows_x[1], masks[2 * p + i])
-        two = pl.ds(2 * p, 2)
-        to_slab(
-            lambda d: slots_out.at[1, two, piece(d), :],
-            lambda d: slots_in.at[1, two, piece(d), :],
-            s2.at[p + 1],
-            r2.at[p + 1],
-        )
-        return carry
-
-    lax.fori_loop(0, 2, pack_values, 0)
+    lax.fori_loop(0, 2, pack_pair(1), 0)
 
     for r in range(ROUNDS):
         onehot_t[r] = token_onehot(columns[:, r : r + 1])
@@ -422,7 +419,7 @@
         sort_rows(2, r)
         return carry
 
-    arrived(slots_in.at[2], r2.at[3])
+    arrived(slots_in.at[2], r2.at[4])
     lax.fori_loop(0, ROUNDS, sort_cots, 0)
 
     def scores_round(r, carry):
@@ -439,8 +436,9 @@
             z_rows[pl.ds(line + 4, 1), :] = totals[:, 128:]
         return carry
 
-    arrived(slots_in.at[0], r2.at[0])
-    lax.fori_loop(0, ROUNDS, scores_round, 0)
+    for p in range(2):
+        arrived(slots_in.at[0, pl.ds(2 * p, 2)], r2.at[p])
+        lax.fori_loop(2 * p, 2 * p + 2, scores_round, 0)
 
     def outputs_round(r):
         sort_rows(1, r)
@@ -456,7 +454,7 @@
             num_out[r, 128 * g : 128 * g + 128, :] = mm(unsort, moved).astype(bf16)
 
     def outputs_pair(p, carry):
-        arrived(slots_in.at[1, pl.ds(2 * p, 2)], r2.at[p + 1])
+        arrived(slots_in.at[1, pl.ds(2 * p, 2)], r2.at[p + 2])
         for i in range(2):
             outputs_round(2 * p + i)
         return carry
@@ -600,11 +598,11 @@
             partner_sent(to_head, k, row_send.at[a, k], s1.at[a + 1])
             partner_sent(to_home, k, back_send.at[a, k], s6.at[a])
     rest = pl.ds(0, 16 * (PEERS - 1))
-    arrived(slots_out.at[0, :, rest, :], s2.at[0])
-    arrived(slots_out.at[2, :, rest, :], s2.at[3])
+    arrived(slots_out.at[2, :, rest, :], s2.at[4])
     for p in range(2):
         two = pl.ds(2 * p, 2)
-        arrived(slots_out.at[1, two, rest, :], s2.at[p + 1])
+        for a in range(2):
+            arrived(slots_out.at[a, two, rest, :], s2.at[2 * a + p])
         arrived(num_out.at[two, rest, :], sn.at[p])
         arrived(grad_out.at[0, two, rest, :], sg.at[p])
     for r in range(ROUNDS):
@@ -661,7 +659,7 @@
         dma((5,)),
         dma((3,)), dma((3,)),
         dma((4, 4)), dma((4, 4)),
-        dma((4,)), dma((4,)),
+        dma((5,)), dma((5,)),
         dma((2,)), dma((2,)),
         dma((6,)), dma((6,)),
         dma((1,)), dma((1,)),

time: 102 us -> 103 us (level); the launches traced: 101 us -> 101 us
  no operation moved by 1% of the time
where the time goes in v5:
time: 103 us; the launch traced here: 101 us
  Pallas kernels  98.1 us (95%)
  local copies, waits for them, and re-layouts  2.26 us (2%)
    pallas_call x1, Pallas kernels, shards(): pl.pallas_call(kernel, out_shape=(jax.ShapeDtypeStruct((128, 256), f32),...  98.1 us
    unnamed x4, local copies, waits for them, and re-layouts  2.26 us

profile of v5, /device:TPU:6, one launch (start us, length us, event | category | flops | bytes accessed | tf_op | source)
XLA Modules:
  0.0 101.0 jit_solution(6139609643071366906)
XLA Ops:
  0.6 98.1 %shard_map.68 = (f32[128,256]{1,0:T(8,128)}, f32[128,256]{1,0:T(8,128)}) custom-call(bf16[128,256]{1,0:T(8,128)(2,1)} %tok.1, bf16[1024,256]{1,0:T(8,128)(2,1)} %key_hbm.1, bf16[1024,256]{1,0:T(8,128)(2,1)} %value_hbm.1, s32[4,4,128]{2,1,0:T(4,128)} %bitcast.1, bf16[128,256]{1,0:T(8,128)(2,1)} %cot_hbm.1), custom_call_target="tpu_custom_call" | custom-call | tf_op jit(solution)/shard_map/pallas_call | solution.py:670
  98.8 0.0 copy-start
  98.8 1.6 %copy.9 = f32[128,256]{1,0:T(8,128)} copy(f32[128,256]{1,0:T(8,128)} %get-tuple-element.4) | data formatting | bytes 262144
  100.4 0.0 copy-done
  100.4 0.7 copy.10
Async XLA Ops:
  98.8 1.6 %copy-start = (f32[128,256]{1,0:T(8,128)S(1)}, f32[128,256]{1,0:T(8,128)}, u32[]{:S(2)}) copy-start(f32[128,256]{1,0:T(8,128)} %get-tuple-element.5) | copy-start | bytes 393220
